TPU v7x, 128 devices: a whole 4x4x4 slice. The times are simulated.
128 devices in a mesh: kx: 8 (over y_hi, z), ky: 16 (over y_lo, x, core).
Axes of the slice: x: 4, y: 4 (y_hi: 2, y_lo: 2; y = y_hi * 2 + y_lo), z: 4, core: 2. Of those that a mesh axis runs over, the one named last changes fastest.
Arguments:
- green: bfloat16 [2, 512, 512, 256], P(None, 'kx', 'ky'), may hold values from -6 to 6
- vertex: bfloat16 [2, 12, 256, 256], replicated, may hold values from -0.078125 to 0.078125
Outputs:
- sigma: float32 [2, 512, 512, 256], P(None, 'kx', 'ky')
All inputs are finite; a program needn't handle non-finite values.
Results may differ from a plain program's by a relative error of at most 0.04.
Values may be sent and summed in bfloat16 or wider, within the bound.
No kernel may reach another device: no remote copies, remote signals or barrier semaphores. Data moves between devices by JAX's collectives and lax.ppermute only.
A program may use at most 128 MiB of HBM per device.

v0:
```python
import math

import jax
import jax.numpy as jnp
from jax import lax
from jax.sharding import PartitionSpec as P


def for_sending(value):

    def short(part):
        return part.astype(jnp.bfloat16) if part.dtype == jnp.float32 else part

    return jax.tree.map(short, value)


def flip_back(values, along_axis):
    return jnp.roll(jnp.flip(values, along_axis), 1, along_axis)


def phase_table(row_count, col_count, period, direction):
    row_index = jnp.arange(row_count, dtype=jnp.int32)
    col_index = jnp.arange(col_count, dtype=jnp.int32)
    product = row_index[:, None] * col_index[None, :] % period
    angles = product.astype(jnp.float32) * (direction * 2.0 * math.pi / period)
    return (jnp.cos(angles), jnp.sin(angles))


def matmul_two(left, right, lowered):
    if lowered:
        return jnp.dot(left.astype(jnp.bfloat16), right, preferred_element_type=jnp.float32)
    return jnp.dot(left, right, precision=lax.Precision.HIGH)


def section_two(values, table, lowered):
    if lowered:
        return jnp.einsum(
            "anm,nb->bam",
            values.astype(jnp.bfloat16),
            table.astype(jnp.bfloat16),
            preferred_element_type=jnp.float32,
        )
    return jnp.einsum("anm,nb->bam", values, table, precision=lax.Precision.HIGH)


def transform(part_re, part_im, along_axis, direction, lowered):
    length = part_re.shape[along_axis]
    first_len = 1 << (length.bit_length() - 1) // 2
    second_len = length // first_len
    moved_re = jnp.moveaxis(part_re, along_axis, 0)
    moved_im = jnp.moveaxis(part_im, along_axis, 0)
    rest_shape = moved_re.shape[1:]
    inner_size = math.prod(rest_shape)
    flat_re = moved_re.reshape(second_len, first_len * inner_size)
    flat_im = moved_im.reshape(second_len, first_len * inner_size)
    cos_q, sin_q = phase_table(second_len, second_len, second_len, direction)
    top_re = matmul_two(cos_q, flat_re, lowered) - matmul_two(sin_q, flat_im, lowered)
    top_im = matmul_two(cos_q, flat_im, lowered) + matmul_two(sin_q, flat_re, lowered)
    top_re = top_re.reshape(second_len, first_len, inner_size)
    top_im = top_im.reshape(second_len, first_len, inner_size)
    twist_c, twist_s = phase_table(second_len, first_len, length, direction)
    mid_re = top_re * twist_c[:, :, None] - top_im * twist_s[:, :, None]
    mid_im = top_re * twist_s[:, :, None] + top_im * twist_c[:, :, None]
    cos_p, sin_p = phase_table(first_len, first_len, first_len, direction)
    out_re = section_two(mid_re, cos_p, lowered) - section_two(mid_im, sin_p, lowered)
    out_im = section_two(mid_im, cos_p, lowered) + section_two(mid_re, sin_p, lowered)
    out_re = jnp.moveaxis(out_re.reshape((length,) + rest_shape), 0, along_axis)
    out_im = jnp.moveaxis(out_im.reshape((length,) + rest_shape), 0, along_axis)
    return (out_re, out_im)


def contract(rows_green, rows_mirror, vertex):
    freqs = rows_green.shape[2]
    bosons = vertex.shape[1]
    padding = ((0, 0), (0, 0), (0, bosons))
    padded_green = jnp.pad(rows_green, padding)
    padded_mirror = jnp.pad(rows_mirror, padding)

    def advance(carry, boson):
        acc_re, acc_im = carry
        left_re = rows_green[0].astype(jnp.float32)
        left_im = rows_green[1].astype(jnp.float32)
        shift_m = lax.dynamic_slice_in_dim(padded_mirror, boson, freqs, 2).astype(jnp.float32)
        shift_g = lax.dynamic_slice_in_dim(padded_green, boson, freqs, 2).astype(jnp.float32)
        bubble_re = (left_re * shift_m[0] - left_im * shift_m[1]).astype(jnp.bfloat16)
        bubble_im = (left_re * shift_m[1] + left_im * shift_m[0]).astype(jnp.bfloat16)
        panel_re = vertex[0, boson].T
        panel_im = vertex[1, boson].T
        block = jnp.concatenate(
            [jnp.concatenate([panel_re, panel_im], 1), jnp.concatenate([-panel_im, panel_re], 1)], 0
        )
        joined = jnp.concatenate([bubble_re, bubble_im], 1)
        product = jnp.dot(joined, block, preferred_element_type=jnp.float32)
        cross_re = product[:, :freqs]
        cross_im = product[:, freqs:]
        acc_re = acc_re + shift_g[0] * cross_re - shift_g[1] * cross_im
        acc_im = acc_im + shift_g[0] * cross_im + shift_g[1] * cross_re
        return ((acc_re, acc_im), None)

    zeros = jnp.zeros((rows_green.shape[1], freqs), jnp.float32)
    totals, unused = lax.scan(advance, (zeros, zeros), jnp.arange(bosons, dtype=jnp.int32))
    return totals


def pair_order(spectrum, groups):
    rows = spectrum.shape[1]
    length = spectrum.shape[2]
    freqs = spectrum.shape[3]
    half = length // 2
    width = half // groups
    lower = spectrum[:, :, :half]
    upper = spectrum[:, :, half:]
    mirrored = jnp.concatenate([upper[:, :, :1], jnp.flip(upper[:, :, 1:], 2)], 2)
    joined = jnp.stack(
        [
            lower.reshape(2, rows, groups, width, freqs),
            mirrored.reshape(2, rows, groups, width, freqs),
        ],
        3,
    )
    return joined.reshape(2, rows, length, freqs)


def natural_order(block, groups):
    rows = block.shape[1]
    length = block.shape[2]
    freqs = block.shape[3]
    half = length // 2
    width = half // groups
    view = block.reshape(2, rows, groups, 2, width, freqs)
    lower = view[:, :, :, 0].reshape(2, rows, half, freqs)
    mirrored = view[:, :, :, 1].reshape(2, rows, half, freqs)
    upper = jnp.concatenate([mirrored[:, :, :1], jnp.flip(mirrored[:, :, 1:], 2)], 2)
    return jnp.concatenate([lower, upper], 2)


def rows_from(stacked):
    length = stacked.shape[2]
    row_re, row_im = transform(stacked[:, 0], stacked[:, 1], 1, 1.0, True)
    return jnp.stack([row_re / length, row_im / length], 1).astype(jnp.bfloat16)


def per_device(green, vertex):
    freqs = green.shape[3]
    length = green.shape[2] * lax.axis_size("ky")
    devices_x = lax.axis_size("kx")
    devices_y = lax.axis_size("ky")
    groups = devices_x * devices_y
    slab_cols = length // groups
    half_cols = slab_cols // 2
    block = lax.all_to_all(green, "ky", split_axis=1, concat_axis=2, tiled=True)
    col_re, col_im = transform(block[0], block[1], 1, 1.0, True)
    spectrum = jnp.stack([col_re, col_im]).astype(jnp.bfloat16)
    columns = pair_order(spectrum, groups)[None]
    spread = rows_from(
        lax.all_to_all(columns, ("kx", "ky"), split_axis=3, concat_axis=2, tiled=True)
    )
    lattice = spread[0]
    swapped = jnp.concatenate([lattice[:, :, half_cols:], lattice[:, :, :half_cols]], 2)
    flat_index = lax.axis_index("kx") * devices_y + lax.axis_index("ky")
    positions = jnp.arange(slab_cols, dtype=jnp.int32)
    keep = jnp.logical_and(flat_index == 0, positions % half_cols == 0)
    mirrored = jnp.where(keep[None, None, :, None], lattice, swapped)
    mirrored = flip_back(mirrored, 1)
    acc_re, acc_im = contract(
        lattice.reshape(2, length * slab_cols, freqs),
        mirrored.reshape(2, length * slab_cols, freqs),
        vertex,
    )
    field_re = acc_re.reshape(length, slab_cols, freqs)
    field_im = acc_im.reshape(length, slab_cols, freqs)
    back_re, back_im = transform(field_re, field_im, 0, -1.0, False)
    outward = jnp.stack([back_re, back_im])
    ordered = natural_order(
        lax.all_to_all(
            outward.astype(jnp.bfloat16), ("kx", "ky"), split_axis=1, concat_axis=2, tiled=True
        ).astype(outward.dtype),
        groups,
    )
    fin_re, fin_im = transform(ordered[0], ordered[1], 1, -1.0, False)
    settled = jnp.stack([fin_re, fin_im]) / length
    return lax.all_to_all(
        for_sending(settled), "ky", split_axis=2, concat_axis=1, tiled=True
    ).astype(settled.dtype)


def solution(mesh):
    placed = (P(None, "kx", "ky", None), P())
    return jax.shard_map(
        per_device, mesh=mesh, in_specs=placed, out_specs=P(None, "kx", "ky", None), check_vma=False
    )
```

profile of v0, /device:TPU:1, one launch (start us, length us, event | category | flops | bytes accessed | tf_op | source)
XLA Modules:
  0.0 618.4 jit_solution(1643525465971191306)
XLA Ops:
  0.0 3.2 copy.95
  3.2 6.8 %all-to-all-start = ((bf16[2,64,32,256]{3,2,0,1:T(8,128)(2,1)}), bf16[2,64,32,256]{3,2,0,1:T(8,128)(2,1)S(1)}, u32[]{:S(2)}, u32[]{:S(2)}) async-start(bf16[2,64,32,256]{3,2,0,1:T(8,128)(2,1)} %copy.95), calls=%async_computation | async-start | bytes 4194304 | tf_op jit(solution)/shard_map/all_to_all | solution.py:151
  10.1 27.6 %all-to-all-done = bf16[2,64,32,256]{3,2,0,1:T(8,128)(2,1)S(1)} async-done(((bf16[2,64,32,256]{3,2,0,1:T(8,128)(2,1)}), bf16[2,64,32,256]{3,2,0,1:T(8,128)(2,1)S(1)}, u32[]{:S(2)}, u32[]{:S(2)}) %all-to-all-start) | async-done | bytes 2097184 | tf_op jit(solution)/shard_map/all_to_all | solution.py:151
  55.7 12.6 %reshape.217 = bf16[512,4,256]{2,1,0:T(4,128)(2,1)S(1)} reshape(bf16[16,32,1024]{2,1,0:T(8,128)(2,1)S(1)} %copy.102) | data formatting | bytes 2097152 | tf_op jit(solution)/shard_map/reshape | solution.py:68
  76.5 9.6 %all-to-all-start.1 = ((bf16[1,2,4,512,256]{4,2,1,0,3:T(4,128)(2,1)}), bf16[1,2,4,512,256]{4,2,1,0,3:T(4,128)(2,1)S(1)}, u32[]{:S(2)}, u32[]{:S(2)}) async-start(bf16[1,2,4,512,256]{4,2,1,0,3:T(4,128)(2,1)} %copy.105), calls=%async_computation.1 | async-start | bytes 4194304 | tf_op jit(solution)/shard_map/all_to_all | solution.py:156
  86.2 30.6 %all-to-all-done.1 = bf16[1,2,4,512,256]{4,2,1,0,3:T(4,128)(2,1)S(1)} async-done(((bf16[1,2,4,512,256]{4,2,1,0,3:T(4,128)(2,1)}), bf16[1,2,4,512,256]{4,2,1,0,3:T(4,128)(2,1)S(1)}, u32[]{:S(2)}, u32[]{:S(2)}) %all-to-all-start.1) | async-done | bytes 2097184 | tf_op jit(solution)/shard_map/all_to_all | solution.py:156
  140.0 2.8 maximum_select_fusion
  147.0 3.6 slice.101
  150.6 2.9 pad_maximum_fusion.2
  161.5 301.7 %while.13 = (s32[]{:T(128)}, f32[2048,256]{1,0:T(8,128)}, f32[2048,256]{1,0:T(8,128)}, s32[12]{0:T(128)S(1)}, bf16[2,2048,268]{2,1,0:T(8,128)(2,1)}, /*index=5*/...) while((s32[]{:T(128)}, f32[2048,256]{1,0:T(8,128)}, ...), condition=%wide.region_1.2_spmd.clone, body=%wide.region_0.1_spmd.clone.sunk | while | flops 1092681728 | bytes 45088976 | solution.py:101
  163.8 6.4 %dynamic-slice_convert_fusion.3 = (f32[2,2048,256]{2,1,0:T(8,128)S(1)}, f32[2,2048,256]{2,1,0:T(8,128)}) fusion(bf16[2,2048,268]{2,1,0:T(8,128)(2,1)} %get-tuple-element.218, s32[]{:T(128)S(6)} %select_n.264, bf16[2,2048,268]{2,1,0:T(8,128)(2,1)} %get-tuple-element.216), kind=kLoop, calls=%fused_computation.18.clone.1 | loop fusion | flops 2097152 | bytes 12582916 | tf_op jit(solution)/shard_map/while/body/eval_jaxpr/convert_element_type | solution.py:83
  174.8 4.5 fusion.291
  179.3 6.3 %fusion.292 = (f32[2048,256]{1,0:T(8,128)}, f32[2048,256]{1,0:T(8,128)}) fusion(f32[2048,256]{1,0:T(8,128)} %get-tuple-element.202, f32[2,2048,256]{2,1,0:T(8,128)} %get-tuple-element.180, f32[2048,512]{1,0:T(8,128)} %fusion.291, pred[]{:T(512)S(6)} %compare.18, f32[2048,256]{1,0:T(8,128)} %get-tuple-element.201), kind=kLoop, calls=%fused_computation.15.clone.1 | loop fusion | flops 5242880 | bytes 16777216 | tf_op jit(solution)/shard_map/while/body/eval_jaxpr/add | solution.py:97
  187.8 6.4 %dynamic-slice_convert_fusion.3 = (f32[2,2048,256]{2,1,0:T(8,128)S(1)}, f32[2,2048,256]{2,1,0:T(8,128)}) fusion(bf16[2,2048,268]{2,1,0:T(8,128)(2,1)} %get-tuple-element.218, s32[]{:T(128)S(6)} %select_n.264, bf16[2,2048,268]{2,1,0:T(8,128)(2,1)} %get-tuple-element.216), kind=kLoop, calls=%fused_computation.18.clone.1 | loop fusion | flops 2097152 | bytes 12582916 | tf_op jit(solution)/shard_map/while/body/eval_jaxpr/convert_element_type | solution.py:83
  198.9 4.5 fusion.291
  203.3 7.5 %fusion.292 = (f32[2048,256]{1,0:T(8,128)}, f32[2048,256]{1,0:T(8,128)}) fusion(f32[2048,256]{1,0:T(8,128)} %get-tuple-element.202, f32[2,2048,256]{2,1,0:T(8,128)} %get-tuple-element.180, f32[2048,512]{1,0:T(8,128)} %fusion.291, pred[]{:T(512)S(6)} %compare.18, f32[2048,256]{1,0:T(8,128)} %get-tuple-element.201), kind=kLoop, calls=%fused_computation.15.clone.1 | loop fusion | flops 5242880 | bytes 16777216 | tf_op jit(solution)/shard_map/while/body/eval_jaxpr/add | solution.py:97
  213.1 6.4 %dynamic-slice_convert_fusion.3 = (f32[2,2048,256]{2,1,0:T(8,128)S(1)}, f32[2,2048,256]{2,1,0:T(8,128)}) fusion(bf16[2,2048,268]{2,1,0:T(8,128)(2,1)} %get-tuple-element.218, s32[]{:T(128)S(6)} %select_n.264, bf16[2,2048,268]{2,1,0:T(8,128)(2,1)} %get-tuple-element.216), kind=kLoop, calls=%fused_computation.18.clone.1 | loop fusion | flops 2097152 | bytes 12582916 | tf_op jit(solution)/shard_map/while/body/eval_jaxpr/convert_element_type | solution.py:83
  224.1 4.5 fusion.291
  228.6 7.5 %fusion.292 = (f32[2048,256]{1,0:T(8,128)}, f32[2048,256]{1,0:T(8,128)}) fusion(f32[2048,256]{1,0:T(8,128)} %get-tuple-element.202, f32[2,2048,256]{2,1,0:T(8,128)} %get-tuple-element.180, f32[2048,512]{1,0:T(8,128)} %fusion.291, pred[]{:T(512)S(6)} %compare.18, f32[2048,256]{1,0:T(8,128)} %get-tuple-element.201), kind=kLoop, calls=%fused_computation.15.clone.1 | loop fusion | flops 5242880 | bytes 16777216 | tf_op jit(solution)/shard_map/while/body/eval_jaxpr/add | solution.py:97
  238.3 6.4 %dynamic-slice_convert_fusion.3 = (f32[2,2048,256]{2,1,0:T(8,128)S(1)}, f32[2,2048,256]{2,1,0:T(8,128)}) fusion(bf16[2,2048,268]{2,1,0:T(8,128)(2,1)} %get-tuple-element.218, s32[]{:T(128)S(6)} %select_n.264, bf16[2,2048,268]{2,1,0:T(8,128)(2,1)} %get-tuple-element.216), kind=kLoop, calls=%fused_computation.18.clone.1 | loop fusion | flops 2097152 | bytes 12582916 | tf_op jit(solution)/shard_map/while/body/eval_jaxpr/convert_element_type | solution.py:83
  249.3 4.5 fusion.291
  253.8 7.5 %fusion.292 = (f32[2048,256]{1,0:T(8,128)}, f32[2048,256]{1,0:T(8,128)}) fusion(f32[2048,256]{1,0:T(8,128)} %get-tuple-element.202, f32[2,2048,256]{2,1,0:T(8,128)} %get-tuple-element.180, f32[2048,512]{1,0:T(8,128)} %fusion.291, pred[]{:T(512)S(6)} %compare.18, f32[2048,256]{1,0:T(8,128)} %get-tuple-element.201), kind=kLoop, calls=%fused_computation.15.clone.1 | loop fusion | flops 5242880 | bytes 16777216 | tf_op jit(solution)/shard_map/while/body/eval_jaxpr/add | solution.py:97
  263.6 6.4 %dynamic-slice_convert_fusion.3 = (f32[2,2048,256]{2,1,0:T(8,128)S(1)}, f32[2,2048,256]{2,1,0:T(8,128)}) fusion(bf16[2,2048,268]{2,1,0:T(8,128)(2,1)} %get-tuple-element.218, s32[]{:T(128)S(6)} %select_n.264, bf16[2,2048,268]{2,1,0:T(8,128)(2,1)} %get-tuple-element.216), kind=kLoop, calls=%fused_computation.18.clone.1 | loop fusion | flops 2097152 | bytes 12582916 | tf_op jit(solution)/shard_map/while/body/eval_jaxpr/convert_element_type | solution.py:83
  274.6 4.5 fusion.291
  279.1 7.5 %fusion.292 = (f32[2048,256]{1,0:T(8,128)}, f32[2048,256]{1,0:T(8,128)}) fusion(f32[2048,256]{1,0:T(8,128)} %get-tuple-element.202, f32[2,2048,256]{2,1,0:T(8,128)} %get-tuple-element.180, f32[2048,512]{1,0:T(8,128)} %fusion.291, pred[]{:T(512)S(6)} %compare.18, f32[2048,256]{1,0:T(8,128)} %get-tuple-element.201), kind=kLoop, calls=%fused_computation.15.clone.1 | loop fusion | flops 5242880 | bytes 16777216 | tf_op jit(solution)/shard_map/while/body/eval_jaxpr/add | solution.py:97
  288.8 6.4 %dynamic-slice_convert_fusion.3 = (f32[2,2048,256]{2,1,0:T(8,128)S(1)}, f32[2,2048,256]{2,1,0:T(8,128)}) fusion(bf16[2,2048,268]{2,1,0:T(8,128)(2,1)} %get-tuple-element.218, s32[]{:T(128)S(6)} %select_n.264, bf16[2,2048,268]{2,1,0:T(8,128)(2,1)} %get-tuple-element.216), kind=kLoop, calls=%fused_computation.18.clone.1 | loop fusion | flops 2097152 | bytes 12582916 | tf_op jit(solution)/shard_map/while/body/eval_jaxpr/convert_element_type | solution.py:83
  299.8 4.5 fusion.291
  304.3 7.5 %fusion.292 = (f32[2048,256]{1,0:T(8,128)}, f32[2048,256]{1,0:T(8,128)}) fusion(f32[2048,256]{1,0:T(8,128)} %get-tuple-element.202, f32[2,2048,256]{2,1,0:T(8,128)} %get-tuple-element.180, f32[2048,512]{1,0:T(8,128)} %fusion.291, pred[]{:T(512)S(6)} %compare.18, f32[2048,256]{1,0:T(8,128)} %get-tuple-element.201), kind=kLoop, calls=%fused_computation.15.clone.1 | loop fusion | flops 5242880 | bytes 16777216 | tf_op jit(solution)/shard_map/while/body/eval_jaxpr/add | solution.py:97
  314.1 6.4 %dynamic-slice_convert_fusion.3 = (f32[2,2048,256]{2,1,0:T(8,128)S(1)}, f32[2,2048,256]{2,1,0:T(8,128)}) fusion(bf16[2,2048,268]{2,1,0:T(8,128)(2,1)} %get-tuple-element.218, s32[]{:T(128)S(6)} %select_n.264, bf16[2,2048,268]{2,1,0:T(8,128)(2,1)} %get-tuple-element.216), kind=kLoop, calls=%fused_computation.18.clone.1 | loop fusion | flops 2097152 | bytes 12582916 | tf_op jit(solution)/shard_map/while/body/eval_jaxpr/convert_element_type | solution.py:83
  325.1 4.5 fusion.291
  329.6 7.5 %fusion.292 = (f32[2048,256]{1,0:T(8,128)}, f32[2048,256]{1,0:T(8,128)}) fusion(f32[2048,256]{1,0:T(8,128)} %get-tuple-element.202, f32[2,2048,256]{2,1,0:T(8,128)} %get-tuple-element.180, f32[2048,512]{1,0:T(8,128)} %fusion.291, pred[]{:T(512)S(6)} %compare.18, f32[2048,256]{1,0:T(8,128)} %get-tuple-element.201), kind=kLoop, calls=%fused_computation.15.clone.1 | loop fusion | flops 5242880 | bytes 16777216 | tf_op jit(solution)/shard_map/while/body/eval_jaxpr/add | solution.py:97
  339.3 6.4 %dynamic-slice_convert_fusion.3 = (f32[2,2048,256]{2,1,0:T(8,128)S(1)}, f32[2,2048,256]{2,1,0:T(8,128)}) fusion(bf16[2,2048,268]{2,1,0:T(8,128)(2,1)} %get-tuple-element.218, s32[]{:T(128)S(6)} %select_n.264, bf16[2,2048,268]{2,1,0:T(8,128)(2,1)} %get-tuple-element.216), kind=kLoop, calls=%fused_computation.18.clone.1 | loop fusion | flops 2097152 | bytes 12582916 | tf_op jit(solution)/shard_map/while/body/eval_jaxpr/convert_element_type | solution.py:83
  350.3 4.5 fusion.291
  354.8 7.5 %fusion.292 = (f32[2048,256]{1,0:T(8,128)}, f32[2048,256]{1,0:T(8,128)}) fusion(f32[2048,256]{1,0:T(8,128)} %get-tuple-element.202, f32[2,2048,256]{2,1,0:T(8,128)} %get-tuple-element.180, f32[2048,512]{1,0:T(8,128)} %fusion.291, pred[]{:T(512)S(6)} %compare.18, f32[2048,256]{1,0:T(8,128)} %get-tuple-element.201), kind=kLoop, calls=%fused_computation.15.clone.1 | loop fusion | flops 5242880 | bytes 16777216 | tf_op jit(solution)/shard_map/while/body/eval_jaxpr/add | solution.py:97
  364.5 6.4 %dynamic-slice_convert_fusion.3 = (f32[2,2048,256]{2,1,0:T(8,128)S(1)}, f32[2,2048,256]{2,1,0:T(8,128)}) fusion(bf16[2,2048,268]{2,1,0:T(8,128)(2,1)} %get-tuple-element.218, s32[]{:T(128)S(6)} %select_n.264, bf16[2,2048,268]{2,1,0:T(8,128)(2,1)} %get-tuple-element.216), kind=kLoop, calls=%fused_computation.18.clone.1 | loop fusion | flops 2097152 | bytes 12582916 | tf_op jit(solution)/shard_map/while/body/eval_jaxpr/convert_element_type | solution.py:83
  375.6 4.5 fusion.291
  380.0 7.5 %fusion.292 = (f32[2048,256]{1,0:T(8,128)}, f32[2048,256]{1,0:T(8,128)}) fusion(f32[2048,256]{1,0:T(8,128)} %get-tuple-element.202, f32[2,2048,256]{2,1,0:T(8,128)} %get-tuple-element.180, f32[2048,512]{1,0:T(8,128)} %fusion.291, pred[]{:T(512)S(6)} %compare.18, f32[2048,256]{1,0:T(8,128)} %get-tuple-element.201), kind=kLoop, calls=%fused_computation.15.clone.1 | loop fusion | flops 5242880 | bytes 16777216 | tf_op jit(solution)/shard_map/while/body/eval_jaxpr/add | solution.py:97
  389.8 6.4 %dynamic-slice_convert_fusion.3 = (f32[2,2048,256]{2,1,0:T(8,128)S(1)}, f32[2,2048,256]{2,1,0:T(8,128)}) fusion(bf16[2,2048,268]{2,1,0:T(8,128)(2,1)} %get-tuple-element.218, s32[]{:T(128)S(6)} %select_n.264, bf16[2,2048,268]{2,1,0:T(8,128)(2,1)} %get-tuple-element.216), kind=kLoop, calls=%fused_computation.18.clone.1 | loop fusion | flops 2097152 | bytes 12582916 | tf_op jit(solution)/shard_map/while/body/eval_jaxpr/convert_element_type | solution.py:83
  400.8 4.5 fusion.291
  405.3 7.5 %fusion.292 = (f32[2048,256]{1,0:T(8,128)}, f32[2048,256]{1,0:T(8,128)}) fusion(f32[2048,256]{1,0:T(8,128)} %get-tuple-element.202, f32[2,2048,256]{2,1,0:T(8,128)} %get-tuple-element.180, f32[2048,512]{1,0:T(8,128)} %fusion.291, pred[]{:T(512)S(6)} %compare.18, f32[2048,256]{1,0:T(8,128)} %get-tuple-element.201), kind=kLoop, calls=%fused_computation.15.clone.1 | loop fusion | flops 5242880 | bytes 16777216 | tf_op jit(solution)/shard_map/while/body/eval_jaxpr/add | solution.py:97
  415.0 6.4 %dynamic-slice_convert_fusion.3 = (f32[2,2048,256]{2,1,0:T(8,128)S(1)}, f32[2,2048,256]{2,1,0:T(8,128)}) fusion(bf16[2,2048,268]{2,1,0:T(8,128)(2,1)} %get-tuple-element.218, s32[]{:T(128)S(6)} %select_n.264, bf16[2,2048,268]{2,1,0:T(8,128)(2,1)} %get-tuple-element.216), kind=kLoop, calls=%fused_computation.18.clone.1 | loop fusion | flops 2097152 | bytes 12582916 | tf_op jit(solution)/shard_map/while/body/eval_jaxpr/convert_element_type | solution.py:83
  426.0 4.5 fusion.291
  430.5 7.5 %fusion.292 = (f32[2048,256]{1,0:T(8,128)}, f32[2048,256]{1,0:T(8,128)}) fusion(f32[2048,256]{1,0:T(8,128)} %get-tuple-element.202, f32[2,2048,256]{2,1,0:T(8,128)} %get-tuple-element.180, f32[2048,512]{1,0:T(8,128)} %fusion.291, pred[]{:T(512)S(6)} %compare.18, f32[2048,256]{1,0:T(8,128)} %get-tuple-element.201), kind=kLoop, calls=%fused_computation.15.clone.1 | loop fusion | flops 5242880 | bytes 16777216 | tf_op jit(solution)/shard_map/while/body/eval_jaxpr/add | solution.py:97
  440.3 6.4 %dynamic-slice_convert_fusion.3 = (f32[2,2048,256]{2,1,0:T(8,128)S(1)}, f32[2,2048,256]{2,1,0:T(8,128)}) fusion(bf16[2,2048,268]{2,1,0:T(8,128)(2,1)} %get-tuple-element.218, s32[]{:T(128)S(6)} %select_n.264, bf16[2,2048,268]{2,1,0:T(8,128)(2,1)} %get-tuple-element.216), kind=kLoop, calls=%fused_computation.18.clone.1 | loop fusion | flops 2097152 | bytes 12582916 | tf_op jit(solution)/shard_map/while/body/eval_jaxpr/convert_element_type | solution.py:83
  451.3 4.5 fusion.291
  455.8 7.5 %fusion.292 = (f32[2048,256]{1,0:T(8,128)}, f32[2048,256]{1,0:T(8,128)}) fusion(f32[2048,256]{1,0:T(8,128)} %get-tuple-element.202, f32[2,2048,256]{2,1,0:T(8,128)} %get-tuple-element.180, f32[2048,512]{1,0:T(8,128)} %fusion.291, pred[]{:T(512)S(6)} %compare.18, f32[2048,256]{1,0:T(8,128)} %get-tuple-element.201), kind=kLoop, calls=%fused_computation.15.clone.1 | loop fusion | flops 5242880 | bytes 16777216 | tf_op jit(solution)/shard_map/while/body/eval_jaxpr/add | solution.py:97
  463.3 2.9 reshape_reshape.6
  466.2 4.1 fusion.47
  471.8 2.8 fusion.46
  487.4 2.6 add_convert_fusion
  493.7 34.9 %all_to_all.51 = bf16[2,512,4,256]{3,2,0,1:T(4,128)(2,1)S(1)} all-to-all(bf16[2,512,4,256]{3,2,0,1:T(4,128)(2,1)S(1)} %copy.113), channel_id=1, replica_groups=mesh['kx'=8,'ky'=16] {'kx','ky'}, dimensions={1} | all-to-all | bytes 4194304 | tf_op jit(solution)/shard_map/all_to_all | solution.py:175
  529.0 2.7 copy.115
  531.7 2.4 copy.116
  537.7 3.3 rev.11
  543.5 2.8 slice_bitcast_fusion.3
  546.2 2.5 reshape.223
  548.7 2.4 fusion.45
  551.1 3.3 reshape.224
  554.4 2.8 fusion.44
  563.5 2.3 fusion.54
  566.9 2.5 copy.119
  569.5 3.3 reshape.227
  572.8 3.5 copy.138
  584.8 30.1 %all_to_all.52 = bf16[2,4,512,256]{3,1,0,2:T(4,128)(2,1)S(1)} all-to-all(bf16[2,4,512,256]{3,1,0,2:T(4,128)(2,1)S(1)} %copy.123), channel_id=1, replica_groups=mesh['kx'=8,'ky'=16] {'ky'}, dimensions={2} | all-to-all | bytes 4194304 | tf_op jit(solution)/shard_map/all_to_all | solution.py:182
  (181 shorter events, 153.2 us)
Async XLA Ops:
  3.2 34.5 %all-to-all-start = ((bf16[2,64,32,256]{3,2,0,1:T(8,128)(2,1)}), bf16[2,64,32,256]{3,2,0,1:T(8,128)(2,1)S(1)}, u32[]{:S(2)}, u32[]{:S(2)}) async-start(bf16[2,64,32,256]{3,2,0,1:T(8,128)(2,1)} %copy.95), calls=%async_computation | async-start | bytes 4194304 | tf_op jit(solution)/shard_map/all_to_all | solution.py:151
  43.3 1.6 copy-start.9
  76.5 40.4 %all-to-all-start.1 = ((bf16[1,2,4,512,256]{4,2,1,0,3:T(4,128)(2,1)}), bf16[1,2,4,512,256]{4,2,1,0,3:T(4,128)(2,1)S(1)}, u32[]{:S(2)}, u32[]{:S(2)}) async-start(bf16[1,2,4,512,256]{4,2,1,0,3:T(4,128)(2,1)} %copy.105), calls=%async_computation.1 | async-start | bytes 4194304 | tf_op jit(solution)/shard_map/all_to_all | solution.py:156
  122.1 1.6 copy-start.10
  142.8 2.1 copy-start.6
  147.0 3.7 slice-start
  155.6 1.9 copy-start.11
  466.2 4.1 copy-start
  471.8 2.8 copy-start.2
  471.8 2.9 copy-start.7
  475.8 1.6 copy-start.1
  490.1 1.4 copy-start.13
  540.9 1.6 copy-start.12
  554.4 2.8 copy-start.3
  554.4 2.9 copy-start.8
  572.8 3.5 copy-start.4
  580.6 2.2 copy-start.5
where the time goes:
time: 629 us; the launch traced here: 618 us
  other arithmetic  213 us (34%)
  local copies, waits for them, and re-layouts  132 us (21%)
  matrix products  99.1 us (16%)
  blocking collectives  65 us (10%)
  waiting for transfers between devices  58.2 us (9%)
  loops' own time  33.7 us (5%)
  starting transfers between devices  16.5 us (3%)
    add x12, other arithmetic, advance(): acc_im = acc_im + shift_g[0] * cross_im + shift_g[1] * cross_re  88.8 us
    convert_element_type x12, other arithmetic, advance(): lax.dynamic_slice_in_dim(padded_mirror, boson, freqs, 2).astype(jnp.float32)  77 us
    dot_general x12, matrix products, advance(): product = jnp.dot(joined, block, preferred_element_type=jnp.float32)  53.8 us
    all_to_all x1, blocking collectives, per_device(): lax.all_to_all(outward.astype(jnp.bfloat16), ('kx', 'ky'), split_axis=1,...  34.9 us
    another operation x1, loops' own time, contract(): lax.scan(advance, (zeros, zeros), jnp.arange(bosons, dtype=jnp.int32))  33.7 us
    all_to_all x1, waiting for transfers between devices, per_device(): lax.all_to_all(columns, ('kx', 'ky'), split_axis=3, concat_axis=2, tiled=...  30.6 us
    all_to_all x1, blocking collectives, per_device(): lax.all_to_all(for_sending(settled), 'ky', split_axis=2, concat_axis=1, t...  30.1 us
    all_to_all x1, waiting for transfers between devices, per_device(): block = lax.all_to_all(green, 'ky', split_axis=1, concat_axis=2, tiled=True)  27.6 us
  transfers between devices with their start and end apart: 2, of which 2 were waited for; matrix products, arithmetic and copies ran while one was open for 0% of the time, Pallas kernels for 0%

commit v1 on v0

v1 whole, which is shorter than its diff:
```python
import math

import jax
import jax.numpy as jnp
import ml_dtypes
import numpy as np
from jax import lax
from jax.experimental import pallas as pl
from jax.experimental.pallas import tpu as pltpu
from jax.sharding import PartitionSpec as P

LANES = 128
ROWS = 256


def pair_list(length):
    half = length // 2
    upper = (length - np.arange(half)) % length
    upper[0] = half
    return np.concatenate([np.arange(half), upper])


def complex_table(sites, momenta, length, direction, scale):
    phase = (sites[:, None].astype(np.int64) * momenta[None, :] % length) * (
        direction * 2.0 * math.pi / length
    )
    cos, sin = np.cos(phase) * scale, np.sin(phase) * scale
    return np.stack([np.stack([cos, -sin], 1), np.stack([sin, cos], 1)], 0)


def tables(length, groups):
    quad = length // groups
    half_quad = quad // 2
    pairs = pair_list(length)
    natural = np.arange(length)
    own = np.stack(
        [pairs[: length // 2].reshape(groups, half_quad), pairs[length // 2 :].reshape(groups, half_quad)], 1
    ).reshape(groups, quad)
    n = 2 * length
    t_y = complex_table(own.T.reshape(-1), natural, length, 1.0, 1.0)
    t_y = t_y.reshape(2, quad, groups, 2, length).transpose(1, 0, 2, 3, 4).reshape(n, n)
    t_x = complex_table(pairs, natural, length, 1.0, 1.0 / length)
    t_x = t_x.reshape(2, length, 2, length).transpose(0, 1, 3, 2).reshape(n, n)
    b_x = complex_table(natural, pairs, length, -1.0, 1.0)
    b_x = b_x.transpose(1, 0, 2, 3).reshape(n, n)
    b_y = complex_table(natural, own.T.reshape(-1), length, -1.0, 1.0 / length)
    b_y = b_y.reshape(2, length, 2, quad, groups).transpose(0, 1, 3, 2, 4).reshape(n, n)
    return [t.astype(ml_dtypes.bfloat16) for t in (t_y, t_x, b_x, b_y)]


def dot(left, right):
    return jnp.dot(left, right, preferred_element_type=jnp.float32)


def columns_kernel(quad, groups, freqs, block_ref, table_ref, out_ref, wide_ref):
    length = quad * groups

    def row(r, carry):
        rhs = jnp.concatenate(
            [block_ref[:, c, r].reshape(length, freqs) for c in range(2)], 0
        )
        for col in range(quad):
            for c in range(2):
                m = (col * 2 + c) * groups
                part = dot(table_ref[m : m + groups, :], rhs)
                for k in range(freqs // LANES):
                    spots = pl.ds(r * 2 + c, groups, stride=2 * quad)
                    wide_ref[col * (freqs // LANES) + k, spots, :] = part[:, k * LANES : (k + 1) * LANES]
        return carry

    lax.fori_loop(0, quad, row, 0)

    def settle(i, carry):
        at = pl.ds(pl.multiple_of(i * 128, 128), 128)
        for k in range(quad * freqs // LANES):
            out_ref[at, k * LANES : (k + 1) * LANES] = wide_ref[k, at, :].astype(jnp.bfloat16)
        return carry

    lax.fori_loop(0, 2 * length // 128, settle, 0)


def shifted(values, by):
    if by == 0:
        return values
    tail = jnp.zeros((values.shape[0], by), values.dtype)
    return jnp.concatenate([values[:, by:], tail], 1)


def sites_kernel(quad, freqs, bosons, spot_ref, block_ref, fore_ref, panel_ref, back_ref, out_ref, green_ref, field_ref):
    length = fore_ref.shape[0] // 2
    half = length // 2
    steps = half // ROWS
    first = spot_ref[0] == 0

    for col in range(quad):
        lanes = slice(col * freqs, (col + 1) * freqs)

        def lattice(i, carry):
            at = pl.ds(pl.multiple_of(i * 256, 256), 256)
            green_ref[col, at, :] = dot(fore_ref[at, :], block_ref[:, lanes]).astype(jnp.bfloat16)
            return carry

        lax.fori_loop(0, 2 * length // 256, lattice, 0)

    def site_block(step, carry):
        col = step // (2 * steps)
        side = (step // steps) % 2
        start = (step % steps) * ROWS
        partner = jnp.where(jnp.logical_and(first, col % 2 == 0), col, (col + quad // 2) % quad)
        here = side * half + start
        there = (1 - side) * half + start
        own_rows = [pl.ds(pl.multiple_of(c * length + here, ROWS), ROWS) for c in range(2)]
        far_rows = [pl.ds(pl.multiple_of(c * length + there, ROWS), ROWS) for c in range(2)]
        g_re = green_ref[col, own_rows[0], :]
        g_im = green_ref[col, own_rows[1], :]
        index = lax.broadcasted_iota(jnp.int32, (ROWS, freqs), 0) + start
        m_re = jnp.where(index == 0, green_ref[partner, own_rows[0], :], green_ref[partner, far_rows[0], :])
        m_im = jnp.where(index == 0, green_ref[partner, own_rows[1], :], green_ref[partner, far_rows[1], :])
        acc_re = jnp.zeros((ROWS, freqs), jnp.float32)
        acc_im = jnp.zeros((ROWS, freqs), jnp.float32)
        for w in range(bosons):
            s_re, s_im = shifted(m_re, w), shifted(m_im, w)
            bubble = jnp.concatenate([g_re * s_re - g_im * s_im, g_re * s_im + g_im * s_re], 1)
            cross = dot(bubble, panel_ref[w]).astype(jnp.bfloat16)
            c_re, c_im = cross[:, :freqs], cross[:, freqs:]
            h_re, h_im = shifted(g_re, w), shifted(g_im, w)
            acc_re = acc_re + (h_re * c_re - h_im * c_im).astype(jnp.float32)
            acc_im = acc_im + (h_re * c_im + h_im * c_re).astype(jnp.float32)
        field_ref[col, own_rows[0], :] = acc_re.astype(jnp.bfloat16)
        field_ref[col, own_rows[1], :] = acc_im.astype(jnp.bfloat16)
        return carry

    lax.fori_loop(0, quad * 2 * steps, site_block, 0)

    for col in range(quad):
        lanes = slice(col * freqs, (col + 1) * freqs)

        def momenta(i, carry):
            at = pl.ds(pl.multiple_of(i * 256, 256), 256)
            out_ref[at, lanes] = dot(back_ref[at, :], field_ref[col]).astype(jnp.bfloat16)
            return carry

        lax.fori_loop(0, 2 * length // 256, momenta, 0)


def rows_kernel(quad, groups, freqs, block_ref, table_ref, out_ref, wide_ref, rhs_ref):
    length = quad * groups
    targets, width = out_ref.shape[0], out_ref.shape[3]

    def widen(i, carry):
        at = pl.ds(pl.multiple_of(i * 128, 128), 128)
        for k in range(quad * freqs // LANES):
            wide_ref[k, at, :] = block_ref[at, k * LANES : (k + 1) * LANES].astype(jnp.float32)
        return carry

    lax.fori_loop(0, 2 * length // 128, widen, 0)

    def row(r, carry):
        for col in range(quad):
            for c in range(2):
                m = (col * 2 + c) * groups
                for k in range(freqs // LANES):
                    part = wide_ref[col * (freqs // LANES) + k, pl.ds(r * 2 + c, groups, stride=2 * quad), :]
                    rhs_ref[m : m + groups, k * LANES : (k + 1) * LANES] = part.astype(jnp.bfloat16)
        for c in range(2):
            for h in range(2):
                at = c * length + h * (length // 2)
                part = dot(table_ref[at : at + length // 2, :], rhs_ref[...])
                out_ref[h * (targets // 2) : (h + 1) * (targets // 2), c, r] = part.reshape(
                    targets // 2, width, freqs
                ).astype(jnp.bfloat16)
        return carry

    lax.fori_loop(0, quad, row, 0)


def in_vmem():
    return pl.BlockSpec(memory_space=pltpu.VMEM)


def call(kernel, out_shape, in_specs, scratch, flops, limit, name):
    return pl.pallas_call(
        kernel,
        out_shape=jax.ShapeDtypeStruct(out_shape, jnp.bfloat16),
        in_specs=in_specs,
        out_specs=in_vmem(),
        scratch_shapes=scratch,
        compiler_params=pltpu.CompilerParams(vmem_limit_bytes=limit * 2**20),
        cost_estimate=pl.CostEstimate(flops=flops, bytes_accessed=2**22, transcendentals=0),
        name=name,
    )


def per_device(green, vertex):
    kx, ky = lax.axis_size("kx"), lax.axis_size("ky")
    groups = kx * ky
    rows, width, freqs = green.shape[1:]
    length = width * ky
    quad = length // groups
    bosons = vertex.shape[1]
    n = 2 * length
    t_y, t_x, b_x, b_y = [jnp.asarray(t) for t in tables(length, groups)]
    both = ("kx", "ky")

    turned = jnp.swapaxes(vertex, 2, 3)
    panels = jnp.concatenate(
        [
            jnp.concatenate([turned[0], turned[1]], 2),
            jnp.concatenate([-turned[1], turned[0]], 2),
        ],
        1,
    )

    block = green.reshape(2, ky, quad, width, freqs).transpose(1, 0, 2, 3, 4)
    block = lax.all_to_all(block, "ky", split_axis=0, concat_axis=0, tiled=True)
    spectrum = call(
        lambda *refs: columns_kernel(quad, groups, freqs, *refs),
        (n, quad * freqs),
        [in_vmem()] * 2,
        [pltpu.VMEM((quad * freqs // LANES, n, LANES), jnp.float32)],
        2 * n * n * quad * freqs,
        16,
        "to_columns",
    )(block, t_y)
    spectrum = lax.all_to_all(spectrum, both, split_axis=0, concat_axis=0, tiled=True)
    spot = (lax.axis_index("kx") * ky + lax.axis_index("ky")).astype(jnp.int32).reshape(1)
    field = call(
        lambda *refs: sites_kernel(quad, freqs, bosons, *refs),
        (n, quad * freqs),
        [pl.BlockSpec(memory_space=pltpu.SMEM)] + [in_vmem()] * 4,
        [
            pltpu.VMEM((quad, n, freqs), jnp.bfloat16),
            pltpu.VMEM((quad, n, freqs), jnp.bfloat16),
        ],
        2 * n * n * quad * freqs * 2 + 8 * bosons * length * quad * freqs * freqs,
        32,
        "on_sites",
    )(spot, spectrum, t_x, panels, b_x)
    field = lax.all_to_all(field, both, split_axis=0, concat_axis=0, tiled=True)
    settled = call(
        lambda *refs: rows_kernel(quad, groups, freqs, *refs),
        (ky, 2, quad, width, freqs),
        [in_vmem()] * 2,
        [pltpu.VMEM((quad * freqs // LANES, n, LANES), jnp.float32), pltpu.VMEM((n, freqs), jnp.bfloat16)],
        2 * n * n * quad * freqs,
        16,
        "to_rows",
    )(field, b_y)
    settled = lax.all_to_all(settled, "ky", split_axis=0, concat_axis=0, tiled=True)
    return settled.transpose(1, 0, 2, 3, 4).reshape(2, rows, width, freqs).astype(jnp.float32)


def solution(mesh):
    placed = (P(None, "kx", "ky", None), P())
    return jax.shard_map(
        per_device, mesh=mesh, in_specs=placed, out_specs=P(None, "kx", "ky", None), check_vma=False
    )
```

time: 629 us -> 185 us (0.29); the launches traced: 618 us -> 185 us
  other arithmetic: 213 us -> 5.18 us
  local copies, waits for them, and re-layouts: 132 us -> 17.1 us
  matrix products: 99.1 us -> 0 us
  waiting for transfers between devices: 58.2 us -> 20.4 us
  Pallas kernels: 0 us -> 35.2 us
  loops' own time: 33.7 us -> 0 us
  blocking collectives: 65 us -> 98.5 us
  starting transfers between devices: 16.5 us -> 8.31 us
    dot_general x44 -> x0, matrix products: 99.1 us -> none  [the longest x12 53.8 us: advance(): product = jnp.dot(joined, block, preferred_element_type=jnp.float32)]
    convert_element_type x29 -> x1, other arithmetic: 98.9 us -> 0.48 us  [per_device(): settled.transpose(1, 0, 2, 3, 4).reshape(2, rows, width, freqs)]
    add x12 -> x0, other arithmetic: 88.8 us -> none  [advance(): acc_im = acc_im + shift_g[0] * cross_im + shift_g[1] * cross_re]
    all_to_all x2 -> x1, waiting for transfers between devices: 58.2 us -> 20.4 us  [per_device(): lax.all_to_all(spectrum, both, split_axis=0, concat_axis=0, tiled=True)]
    pallas_call x0 -> x3, Pallas kernels: none -> 35.2 us  [the longest x1 27.8 us: per_device(): call(lambda *refs: sites_kernel(quad, freqs, bosons, *refs), (n, quad * f...]
    another operation x1 -> x0, loops' own time: 33.7 us -> none  [contract(): lax.scan(advance, (zeros, zeros), jnp.arange(bosons, dtype=jnp.int32))]
    all_to_all x2 -> x3, blocking collectives: 65 us -> 98.5 us  [the longest x1 34.9 us: per_device(): field = lax.all_to_all(field, both, split_axis=0, concat_axis=0, tiled=True)]
    reshape x11 -> x1, local copies, waits for them, and re-layouts: 33.8 us -> 1.76 us  [per_device(): block = green.reshape(2, ky, quad, width, freqs).transpose(1, 0, 2, 3, 4)]
  transfers between devices with their start and end apart: 2 -> 1, of which waited for: 2 -> 1; matrix products, arithmetic and copies ran while one was open for 0% -> 5% of each run, Pallas kernels for 0% -> 0%
where the time goes in v1:
time: 185 us
  blocking collectives  98.5 us (53%)
  Pallas kernels  35.2 us (19%)
  waiting for transfers between devices  20.4 us (11%)
  local copies, waits for them, and re-layouts  17.1 us (9%)
  starting transfers between devices  8.31 us (4%)
  other arithmetic  5.18 us (3%)
    all_to_all x1, blocking collectives, per_device(): field = lax.all_to_all(field, both, split_axis=0, concat_axis=0, tiled=True)  34.9 us
    all_to_all x1, blocking collectives, per_device(): block = lax.all_to_all(block, 'ky', split_axis=0, concat_axis=0, tiled=True)  33.5 us
    all_to_all x1, blocking collectives, per_device(): lax.all_to_all(settled, 'ky', split_axis=0, concat_axis=0, tiled=True)  30.1 us
    pallas_call x1, Pallas kernels, per_device(): call(lambda *refs: sites_kernel(quad, freqs, bosons, *refs), (n, quad * f...  27.8 us
    all_to_all x1, waiting for transfers between devices, per_device(): lax.all_to_all(spectrum, both, split_axis=0, concat_axis=0, tiled=True)  20.4 us
    unnamed x15, local copies, waits for them, and re-layouts  12.7 us
    all_to_all x1, starting transfers between devices, per_device(): lax.all_to_all(spectrum, both, split_axis=0, concat_axis=0, tiled=True)  8.31 us
    pallas_call x1, Pallas kernels, per_device(): call(lambda *refs: rows_kernel(quad, groups, freqs, *refs), (ky, 2, quad,...  3.93 us
  transfers between devices with their start and end apart: 1, of which 1 were waited for; matrix products, arithmetic and copies ran while one was open for 5% of the time, Pallas kernels for 0%

profile of v1, /device:TPU:1, one launch (start us, length us, event | category | flops | bytes accessed | tf_op | source)
XLA Modules:
  0.0 184.7 jit_solution(2979071161546603199)
XLA Ops:
  0.0 1.8 copy.12
  1.8 0.0 copy-start.5
  1.8 33.5 %all_to_all.32.refs_0_ = bf16[16,2,4,32,256]{4,3,2,1,0:T(8,128)(2,1)S(1)} all-to-all(bf16[16,2,4,32,256]{4,3,2,1,0:T(8,128)(2,1)S(1)} %bitcast.25), channel_id=1, replica_groups=mesh['kx'=8,'ky'=16] {'ky'}, dimensions={0} | all-to-all | bytes 4194304 | tf_op jit(solution)/shard_map/all_to_all | solution.py:215
  35.3 0.0 copy-done.5
  35.3 3.4 %to_columns.1 = bf16[1024,1024]{1,0:T(8,128)(2,1)S(1)} custom-call(bf16[16,2,4,32,256]{4,3,2,1,0:T(8,128)(2,1)S(1)} %all_to_all.32.refs_0_, bf16[1024,1024]{1,0:T(8,128)(2,1)S(1)} %copy-done.5), custom_call_target="tpu_custom_call" | custom-call | flops 2147483648 | bytes 4194304 | tf_op jit(solution)/shard_map/to_columns/pallas_call | solution.py:216
  38.7 0.0 copy-start.1
  38.7 1.3 copy-done.1
  40.1 8.3 %all-to-all-start.1 = ((bf16[128,8,1024]{2,1,0:T(8,128)(2,1)}), bf16[128,8,1024]{2,1,0:T(8,128)(2,1)S(1)}, u32[]{:S(2)}, u32[]{:S(2)}) async-start(bf16[128,8,1024]{2,1,0:T(8,128)(2,1)} %bitcast.20), calls=%async_computation.1 | async-start | bytes 4194304 | tf_op jit(solution)/shard_map/all_to_all | solution.py:225
  48.4 4.6 %copy.9 = bf16[2,12,256,256]{2,3,1,0:T(8,128)(2,1)} copy(bf16[2,12,256,256]{3,2,1,0:T(8,128)(2,1)} %param.7) | data formatting | bytes 6291456 | tf_op args[1]
  53.0 0.0 copy-start.6
  53.0 1.7 fusion
  54.7 0.7 copy-done.6
  55.4 0.3 slice_bitcast_fusion
  55.7 3.0 %maximum_maximum_fusion.refs_3_ = bf16[12,512,512]{2,1,0:T(8,128)(2,1)} fusion(bf16[12,256,256]{2,1,0:T(8,128)(2,1)S(1)} %get-tuple-element.6, bf16[12,256,256]{2,1,0:T(8,128)(2,1)S(1)} %fusion, bf16[12,256,256]{2,1,0:T(8,128)(2,1)S(1)} %get-tuple-element.5), kind=kLoop, calls=%fused_computation | loop fusion | flops 25165824 | bytes 11010048 | tf_op jit(solution)/shard_map/concatenate | solution.py:206
  58.7 20.4 %all-to-all-done.1 = bf16[128,8,1024]{2,1,0:T(8,128)(2,1)S(1)} async-done(((bf16[128,8,1024]{2,1,0:T(8,128)(2,1)}), bf16[128,8,1024]{2,1,0:T(8,128)(2,1)S(1)}, u32[]{:S(2)}, u32[]{:S(2)}) %all-to-all-start.1) | async-done | bytes 2097184 | tf_op jit(solution)/shard_map/all_to_all | solution.py:225
  79.1 0.0 copy-start
  79.1 2.8 %copy-done = bf16[12,512,512]{2,1,0:T(8,128)(2,1)S(1)} copy-done((bf16[12,512,512]{2,1,0:T(8,128)(2,1)S(1)}, bf16[12,512,512]{2,1,0:T(8,128)(2,1)}, u32[]{:S(2)}) %copy-start) | copy-done | bytes 6291480
  81.9 0.0 copy-start.3
  81.9 1.6 copy-done.3
  83.5 0.0 copy-start.4
  83.5 1.6 copy-done.4
  85.1 27.8 %on_sites.1 = bf16[1024,1024]{1,0:T(8,128)(2,1)S(1)} custom-call(s32[1]{0:T(128)} %bitcast.refs_0_, bf16[1024,1024]{1,0:T(8,128)(2,1)S(1)} %bitcast.19, bf16[1024,1024]{1,0:T(8,128)(2,1)S(1)} %copy-done.3, bf16[12,512,512]{2,1,0:T(8,128)(2,1)S(1)} %copy-done, bf16[1024,1024]{1,0:T(8,128)(2,1)S(1)} %copy-done.4), custom_call_target="tpu_custom_call" | custom-call | flops 17179869184 | bytes 4194304 | tf_op jit(solution)/shard_map/on_sites/pallas_call | solution.py:227
  112.9 0.0 copy-start.2
  112.9 34.9 %all_to_all.33 = bf16[128,8,1024]{2,1,0:T(8,128)(2,1)S(1)} all-to-all(bf16[128,8,1024]{2,1,0:T(8,128)(2,1)S(1)} %bitcast.21), channel_id=1, replica_groups=mesh['kx'=8,'ky'=16] {'kx','ky'}, dimensions={0} | all-to-all | bytes 4194304 | tf_op jit(solution)/shard_map/all_to_all | solution.py:239
  147.9 0.0 copy-done.2
  147.9 3.9 %to_rows.1 = bf16[16,2,4,32,256]{4,3,2,1,0:T(8,128)(2,1)S(1)} custom-call(bf16[1024,1024]{1,0:T(8,128)(2,1)S(1)} %bitcast.22, bf16[1024,1024]{1,0:T(8,128)(2,1)S(1)} %copy-done.2), custom_call_target="tpu_custom_call" | custom-call | flops 2147483648 | bytes 4194304 | tf_op jit(solution)/shard_map/to_rows/pallas_call | solution.py:240
  151.8 30.1 %all_to_all.34 = bf16[16,2,4,32,256]{4,3,2,1,0:T(8,128)(2,1)S(1)} all-to-all(bf16[16,2,4,32,256]{4,3,2,1,0:T(8,128)(2,1)S(1)} %to_rows.1), channel_id=1, replica_groups=mesh['kx'=8,'ky'=16] {'ky'}, dimensions={0} | all-to-all | bytes 4194304 | tf_op jit(solution)/shard_map/all_to_all | solution.py:249
  181.9 0.5 convert_bitcast_fusion
  182.4 2.3 %copy.10 = f32[2,16,4,32,256]{4,3,2,1,0:T(8,128)} copy(f32[2,16,4,32,256]{4,3,2,0,1:T(8,128)S(1)} %convert_bitcast_fusion) | data formatting | bytes 8388608 | tf_op jit(solution)/shard_map/convert_element_type | solution.py:250
Async XLA Ops:
  1.8 33.5 %copy-start.5 = (bf16[1024,1024]{1,0:T(8,128)(2,1)S(1)}, bf16[1024,1024]{1,0:T(8,128)(2,1)}, u32[]{:S(2)}) copy-start(bf16[1024,1024]{1,0:T(8,128)(2,1)} %constant.19.clone.refs_1_) | copy-start | bytes 6291460
  38.7 1.4 copy-start.1
  40.1 39.0 %all-to-all-start.1 = ((bf16[128,8,1024]{2,1,0:T(8,128)(2,1)}), bf16[128,8,1024]{2,1,0:T(8,128)(2,1)S(1)}, u32[]{:S(2)}, u32[]{:S(2)}) async-start(bf16[128,8,1024]{2,1,0:T(8,128)(2,1)} %bitcast.20), calls=%async_computation.1 | async-start | bytes 4194304 | tf_op jit(solution)/shard_map/all_to_all | solution.py:225
  53.0 2.4 %copy-start.6 = (bf16[2,12,256,256]{2,3,1,0:T(8,128)(2,1)S(1)}, bf16[2,12,256,256]{2,3,1,0:T(8,128)(2,1)}, u32[]{:S(2)}) copy-start(bf16[2,12,256,256]{2,3,1,0:T(8,128)(2,1)} %copy.9) | copy-start | bytes 9437188
  79.1 2.8 %copy-start = (bf16[12,512,512]{2,1,0:T(8,128)(2,1)S(1)}, bf16[12,512,512]{2,1,0:T(8,128)(2,1)}, u32[]{:S(2)}) copy-start(bf16[12,512,512]{2,1,0:T(8,128)(2,1)} %maximum_maximum_fusion.refs_3_) | copy-start | bytes 18874372
  81.9 1.6 copy-start.3
  83.5 1.6 copy-start.4
  112.9 35.0 %copy-start.2 = (bf16[1024,1024]{1,0:T(8,128)(2,1)S(1)}, bf16[1024,1024]{1,0:T(8,128)(2,1)}, u32[]{:S(2)}) copy-start(bf16[1024,1024]{1,0:T(8,128)(2,1)} %constant.22.clone.refs_1_) | copy-start | bytes 6291460

commit v2 on v1

--- a/solution.py
+++ b/solution.py
@@ -10,7 +10,8 @@
 from jax.sharding import PartitionSpec as P
 
 LANES = 128
-ROWS = 256
+TILE = 16
+GROUP = 4
 
 
 def pair_list(length):
@@ -52,17 +53,19 @@
     return jnp.dot(left, right, preferred_element_type=jnp.float32)
 
 
-def columns_kernel(quad, groups, freqs, block_ref, table_ref, out_ref, wide_ref):
+def columns_kernel(quad, groups, freqs, block_ref, table_ref, panel_hbm, out_ref, wide_ref):
+    del panel_hbm
     length = quad * groups
 
     def row(r, carry):
         rhs = jnp.concatenate(
             [block_ref[:, c, r].reshape(length, freqs) for c in range(2)], 0
         )
+        product = dot(table_ref[...], rhs)
         for col in range(quad):
             for c in range(2):
                 m = (col * 2 + c) * groups
-                part = dot(table_ref[m : m + groups, :], rhs)
+                part = product[m : m + groups]
                 for k in range(freqs // LANES):
                     spots = pl.ds(r * 2 + c, groups, stride=2 * quad)
                     wide_ref[col * (freqs // LANES) + k, spots, :] = part[:, k * LANES : (k + 1) * LANES]
@@ -86,61 +89,93 @@
     return jnp.concatenate([values[:, by:], tail], 1)
 
 
-def sites_kernel(quad, freqs, bosons, spot_ref, block_ref, fore_ref, panel_ref, back_ref, out_ref, green_ref, field_ref):
-    length = fore_ref.shape[0] // 2
-    half = length // 2
-    steps = half // ROWS
+def swap_first(ref, col, c):
+    low, high = ref[col, 2 * c, :TILE, :], ref[col, 2 * c + 1, :TILE, :]
+    top = lax.broadcasted_iota(jnp.int32, low.shape, 0) == 0
+    ref[col, 2 * c, :TILE, :] = jnp.where(top, high, low)
+    ref[col, 2 * c + 1, :TILE, :] = jnp.where(top, low, high)
+
+
+def sites_kernel(
+    quad, freqs, bosons, spot_ref, block_ref, fore_hbm, panel_hbm, back_hbm, out_ref,
+    fore_ref, panel_ref, back_ref, green_ref, field_ref, fore_sem, panel_sem, back_sem,
+):
+    half = green_ref.shape[2]
     first = spot_ref[0] == 0
-
+    fore = [
+        pltpu.make_async_copy(fore_hbm.at[pl.ds(i * half, half)], fore_ref.at[pl.ds(i * half, half)], fore_sem.at[i])
+        for i in range(4)
+    ]
+    for copy in fore:
+        copy.start()
+    panel = pltpu.make_async_copy(panel_hbm, panel_ref, panel_sem)
+    panel.start()
+    back = pltpu.make_async_copy(back_hbm, back_ref, back_sem)
+    back.start()
+
+    for i in range(4):
+        fore[i].wait()
+        lattice = dot(fore_ref[i * half : (i + 1) * half, :], block_ref[...]).astype(jnp.bfloat16)
+        for col in range(quad):
+            green_ref[col, i] = lattice[:, col * freqs : (col + 1) * freqs]
+    for col in range(quad // 2, quad):
+        for c in range(2):
+            swap_first(green_ref, col, c)
+    panel.wait()
+
+    def pair_block(step, carry):
+        column, side = step // 2, step % 2
+        alone = jnp.logical_and(first, column == 0)
+        p_col = jnp.where(alone, side * (quad // 2), column)
+        q_col = jnp.where(alone, side * (quad // 2), column + quad // 2)
+        p_re, p_im = green_ref[p_col, side], green_ref[p_col, 2 + side]
+        q_re, q_im = green_ref[q_col, 1 - side], green_ref[q_col, 3 - side]
+        row = lax.broadcasted_iota(jnp.int32, (TILE, freqs), 0)
+        own = jnp.logical_and(row == 0, alone)
+
+        def mirror(mine, other):
+            return jnp.concatenate([jnp.where(own, mine[:TILE], other[:TILE]), other[TILE:]], 0)
+
+        totals = [jnp.zeros((half, freqs), jnp.float32) for _ in range(4)]
+        for start in range(0, bosons, GROUP):
+            sums = None
+            for w in range(start, min(start + GROUP, bosons)):
+                sp_re, sp_im = shifted(p_re, w), shifted(p_im, w)
+                sq_re, sq_im = shifted(q_re, w), shifted(q_im, w)
+                lefts = []
+                for g_re, g_im, m_re, m_im in (
+                    (p_re, p_im, mirror(sp_re, sq_re), mirror(sp_im, sq_im)),
+                    (q_re, q_im, mirror(sq_re, sp_re), mirror(sq_im, sp_im)),
+                ):
+                    b_re = g_re * m_re - g_im * m_im
+                    b_im = g_re * m_im + g_im * m_re
+                    lefts += [jnp.concatenate([b_re, -b_im], 1), jnp.concatenate([b_im, b_re], 1)]
+                cross = dot(jnp.concatenate(lefts, 0), panel_ref[w]).astype(jnp.bfloat16)
+                cp_re, cp_im, cq_re, cq_im = [cross[i * half : (i + 1) * half] for i in range(4)]
+                terms = [
+                    sp_re * cp_re - sp_im * cp_im,
+                    sp_re * cp_im + sp_im * cp_re,
+                    sq_re * cq_re - sq_im * cq_im,
+                    sq_re * cq_im + sq_im * cq_re,
+                ]
+                sums = terms if sums is None else [s + t for s, t in zip(sums, terms)]
+            totals = [t + s.astype(jnp.float32) for t, s in zip(totals, sums)]
+        p_sum_re, p_sum_im, q_sum_re, q_sum_im = [t.astype(jnp.bfloat16) for t in totals]
+        field_ref[p_col, side] = p_sum_re
+        field_ref[p_col, 2 + side] = p_sum_im
+        field_ref[q_col, 1 - side] = q_sum_re
+        field_ref[q_col, 3 - side] = q_sum_im
+        return carry
+
+    lax.fori_loop(0, quad, pair_block, 0)
+
+    for col in range(quad // 2, quad):
+        for c in range(2):
+            swap_first(field_ref, col, c)
+    back.wait()
     for col in range(quad):
-        lanes = slice(col * freqs, (col + 1) * freqs)
-
-        def lattice(i, carry):
-            at = pl.ds(pl.multiple_of(i * 256, 256), 256)
-            green_ref[col, at, :] = dot(fore_ref[at, :], block_ref[:, lanes]).astype(jnp.bfloat16)
-            return carry
-
-        lax.fori_loop(0, 2 * length // 256, lattice, 0)
-
-    def site_block(step, carry):
-        col = step // (2 * steps)
-        side = (step // steps) % 2
-        start = (step % steps) * ROWS
-        partner = jnp.where(jnp.logical_and(first, col % 2 == 0), col, (col + quad // 2) % quad)
-        here = side * half + start
-        there = (1 - side) * half + start
-        own_rows = [pl.ds(pl.multiple_of(c * length + here, ROWS), ROWS) for c in range(2)]
-        far_rows = [pl.ds(pl.multiple_of(c * length + there, ROWS), ROWS) for c in range(2)]
-        g_re = green_ref[col, own_rows[0], :]
-        g_im = green_ref[col, own_rows[1], :]
-        index = lax.broadcasted_iota(jnp.int32, (ROWS, freqs), 0) + start
-        m_re = jnp.where(index == 0, green_ref[partner, own_rows[0], :], green_ref[partner, far_rows[0], :])
-        m_im = jnp.where(index == 0, green_ref[partner, own_rows[1], :], green_ref[partner, far_rows[1], :])
-        acc_re = jnp.zeros((ROWS, freqs), jnp.float32)
-        acc_im = jnp.zeros((ROWS, freqs), jnp.float32)
-        for w in range(bosons):
-            s_re, s_im = shifted(m_re, w), shifted(m_im, w)
-            bubble = jnp.concatenate([g_re * s_re - g_im * s_im, g_re * s_im + g_im * s_re], 1)
-            cross = dot(bubble, panel_ref[w]).astype(jnp.bfloat16)
-            c_re, c_im = cross[:, :freqs], cross[:, freqs:]
-            h_re, h_im = shifted(g_re, w), shifted(g_im, w)
-            acc_re = acc_re + (h_re * c_re - h_im * c_im).astype(jnp.float32)
-            acc_im = acc_im + (h_re * c_im + h_im * c_re).astype(jnp.float32)
-        field_ref[col, own_rows[0], :] = acc_re.astype(jnp.bfloat16)
-        field_ref[col, own_rows[1], :] = acc_im.astype(jnp.bfloat16)
-        return carry
-
-    lax.fori_loop(0, quad * 2 * steps, site_block, 0)
-
-    for col in range(quad):
-        lanes = slice(col * freqs, (col + 1) * freqs)
-
-        def momenta(i, carry):
-            at = pl.ds(pl.multiple_of(i * 256, 256), 256)
-            out_ref[at, lanes] = dot(back_ref[at, :], field_ref[col]).astype(jnp.bfloat16)
-            return carry
-
-        lax.fori_loop(0, 2 * length // 256, momenta, 0)
+        stacked = field_ref[col].reshape(4 * half, freqs)
+        out_ref[:, col * freqs : (col + 1) * freqs] = dot(back_ref[...], stacked).astype(jnp.bfloat16)
 
 
 def rows_kernel(quad, groups, freqs, block_ref, table_ref, out_ref, wide_ref, rhs_ref):
@@ -162,13 +197,10 @@
                 for k in range(freqs // LANES):
                     part = wide_ref[col * (freqs // LANES) + k, pl.ds(r * 2 + c, groups, stride=2 * quad), :]
                     rhs_ref[m : m + groups, k * LANES : (k + 1) * LANES] = part.astype(jnp.bfloat16)
+        product = dot(table_ref[...], rhs_ref[...]).astype(jnp.bfloat16)
         for c in range(2):
-            for h in range(2):
-                at = c * length + h * (length // 2)
-                part = dot(table_ref[at : at + length // 2, :], rhs_ref[...])
-                out_ref[h * (targets // 2) : (h + 1) * (targets // 2), c, r] = part.reshape(
-                    targets // 2, width, freqs
-                ).astype(jnp.bfloat16)
+            part = product[c * length : (c + 1) * length]
+            out_ref[:, c, r] = part.reshape(targets, width, freqs)
         return carry
 
     lax.fori_loop(0, quad, row, 0)
@@ -202,38 +234,37 @@
     t_y, t_x, b_x, b_y = [jnp.asarray(t) for t in tables(length, groups)]
     both = ("kx", "ky")
 
-    turned = jnp.swapaxes(vertex, 2, 3)
-    panels = jnp.concatenate(
-        [
-            jnp.concatenate([turned[0], turned[1]], 2),
-            jnp.concatenate([-turned[1], turned[0]], 2),
-        ],
-        1,
-    )
+    panels = vertex.transpose(1, 0, 3, 2).reshape(bosons, 2 * freqs, freqs)
 
     block = green.reshape(2, ky, quad, width, freqs).transpose(1, 0, 2, 3, 4)
     block = lax.all_to_all(block, "ky", split_axis=0, concat_axis=0, tiled=True)
     spectrum = call(
         lambda *refs: columns_kernel(quad, groups, freqs, *refs),
         (n, quad * freqs),
-        [in_vmem()] * 2,
+        [in_vmem()] * 2 + [pl.BlockSpec(memory_space=pltpu.HBM)],
         [pltpu.VMEM((quad * freqs // LANES, n, LANES), jnp.float32)],
         2 * n * n * quad * freqs,
         16,
         "to_columns",
-    )(block, t_y)
+    )(block, t_y, panels)
     spectrum = lax.all_to_all(spectrum, both, split_axis=0, concat_axis=0, tiled=True)
     spot = (lax.axis_index("kx") * ky + lax.axis_index("ky")).astype(jnp.int32).reshape(1)
     field = call(
         lambda *refs: sites_kernel(quad, freqs, bosons, *refs),
         (n, quad * freqs),
-        [pl.BlockSpec(memory_space=pltpu.SMEM)] + [in_vmem()] * 4,
+        [pl.BlockSpec(memory_space=pltpu.SMEM), in_vmem()] + [pl.BlockSpec(memory_space=pltpu.HBM)] * 3,
         [
-            pltpu.VMEM((quad, n, freqs), jnp.bfloat16),
-            pltpu.VMEM((quad, n, freqs), jnp.bfloat16),
+            pltpu.VMEM((n, n), jnp.bfloat16),
+            pltpu.VMEM((bosons, 2 * freqs, freqs), jnp.bfloat16),
+            pltpu.VMEM((n, n), jnp.bfloat16),
+            pltpu.VMEM((quad, 4, length // 2, freqs), jnp.bfloat16),
+            pltpu.VMEM((quad, 4, length // 2, freqs), jnp.bfloat16),
+            pltpu.SemaphoreType.DMA((4,)),
+            pltpu.SemaphoreType.DMA,
+            pltpu.SemaphoreType.DMA,
         ],
         2 * n * n * quad * freqs * 2 + 8 * bosons * length * quad * freqs * freqs,
-        32,
+        36,
         "on_sites",
     )(spot, spectrum, t_x, panels, b_x)
     field = lax.all_to_all(field, both, split_axis=0, concat_axis=0, tiled=True)

time: 185 us -> 187 us (1.011)
  waiting for transfers between devices: 20.4 us -> 54.9 us
  blocking collectives: 98.5 us -> 65 us
  starting transfers between devices: 8.31 us -> 17 us
  other arithmetic: 5.18 us -> 0.48 us
  local copies, waits for them, and re-layouts: 17.1 us -> 14.8 us
    all_to_all x1 -> x0, blocking collectives: 33.5 us -> none  [per_device(): block = lax.all_to_all(block, 'ky', split_axis=0, concat_axis=0, tiled=True)]
    all_to_all x0 -> x1, waiting for transfers between devices: none -> 24.5 us  [per_device(): block = lax.all_to_all(block, 'ky', split_axis=0, concat_axis=0, tiled=True)]
    all_to_all x1, waiting for transfers between devices: 20.4 us -> 30.4 us  [per_device(): lax.all_to_all(spectrum, both, split_axis=0, concat_axis=0, tiled=True)]
    all_to_all x0 -> x1, starting transfers between devices: none -> 6.83 us  [per_device(): block = lax.all_to_all(block, 'ky', split_axis=0, concat_axis=0, tiled=True)]
    unnamed x15 -> x10, local copies, waits for them, and re-layouts: 12.7 us -> 6.09 us
    transpose x0 -> x1, local copies, waits for them, and re-layouts: none -> 3.19 us  [per_device(): panels = vertex.transpose(1, 0, 3, 2).reshape(bosons, 2 * freqs, freqs)]
    concatenate x1 -> x0, other arithmetic: 3.04 us -> none  [per_device(): jnp.concatenate([jnp.concatenate([turned[0], turned[1]], 2), jnp.concaten...]
    pallas_call x1, Pallas kernels: 27.8 us -> 25 us  [per_device(): call(lambda *refs: sites_kernel(quad, freqs, bosons, *refs), (n, quad * f...]
  transfers between devices with their start and end apart: 1 -> 2, of which waited for: 1 -> 2; matrix products, arithmetic and copies ran while one was open for 5% -> 2% of each run, Pallas kernels for 0% -> 0%
where the time goes in v2:
time: 187 us; the launch traced here: 186 us
  blocking collectives  65 us (35%)
  waiting for transfers between devices  54.9 us (29%)
  Pallas kernels  34.1 us (18%)
  starting transfers between devices  17 us (9%)
  local copies, waits for them, and re-layouts  14.8 us (8%)
    all_to_all x1, blocking collectives, per_device(): field = lax.all_to_all(field, both, split_axis=0, concat_axis=0, tiled=True)  34.9 us
    all_to_all x1, waiting for transfers between devices, per_device(): lax.all_to_all(spectrum, both, split_axis=0, concat_axis=0, tiled=True)  30.4 us
    all_to_all x1, blocking collectives, per_device(): lax.all_to_all(settled, 'ky', split_axis=0, concat_axis=0, tiled=True)  30.1 us
    pallas_call x1, Pallas kernels, per_device(): call(lambda *refs: sites_kernel(quad, freqs, bosons, *refs), (n, quad * f...  25 us
    all_to_all x1, waiting for transfers between devices, per_device(): block = lax.all_to_all(block, 'ky', split_axis=0, concat_axis=0, tiled=True)  24.5 us
    all_to_all x1, starting transfers between devices, per_device(): lax.all_to_all(spectrum, both, split_axis=0, concat_axis=0, tiled=True)  10.2 us
    all_to_all x1, starting transfers between devices, per_device(): block = lax.all_to_all(block, 'ky', split_axis=0, concat_axis=0, tiled=True)  6.83 us
    unnamed x10, local copies, waits for them, and re-layouts  6.09 us
  transfers between devices with their start and end apart: 2, of which 2 were waited for; matrix products, arithmetic and copies ran while one was open for 2% of the time, Pallas kernels for 0%

profile of v2, /device:TPU:1, one launch (start us, length us, event | category | flops | bytes accessed | tf_op | source)
XLA Modules:
  0.0 186.4 jit_solution(14301000728074388568)
XLA Ops:
  0.0 3.2 %copy.12 = bf16[2,16,4,32,256]{4,3,2,0,1:T(8,128)(2,1)} copy(bf16[2,16,4,32,256]{4,3,2,1,0:T(8,128)(2,1)} %bitcast.20) | data formatting | bytes 4194304 | tf_op jit(solution)/shard_map/reshape | solution.py:239
  3.2 6.8 %all-to-all-start = ((bf16[16,2,4,32,256]{4,3,2,1,0:T(8,128)(2,1)}), bf16[16,2,4,32,256]{4,3,2,1,0:T(8,128)(2,1)}, u32[]{:S(2)}, u32[]{:S(2)}) async-start(bf16[16,2,4,32,256]{4,3,2,1,0:T(8,128)(2,1)} %bitcast.13), calls=%async_computation | async-start | bytes 4194304 | tf_op jit(solution)/shard_map/all_to_all | solution.py:240
  10.0 3.2 %copy.9 = bf16[12,2,256,256]{3,2,1,0:T(8,128)(2,1)S(1)} copy(bf16[12,2,256,256]{2,3,0,1:T(8,128)(2,1)} %bitcast.19) | data formatting | bytes 6291456 | tf_op jit(solution)/shard_map/transpose | solution.py:237
  13.2 24.5 %all-to-all-done.refs_0_ = bf16[16,2,4,32,256]{4,3,2,1,0:T(8,128)(2,1)} async-done(((bf16[16,2,4,32,256]{4,3,2,1,0:T(8,128)(2,1)}), bf16[16,2,4,32,256]{4,3,2,1,0:T(8,128)(2,1)}, u32[]{:S(2)}, u32[]{:S(2)}) %all-to-all-start) | async-done | bytes 2097184 | tf_op jit(solution)/shard_map/all_to_all | solution.py:240
  37.7 0.0 copy-start.1
  37.7 1.6 copy-done.1
  39.3 5.0 %to_columns.1 = bf16[1024,1024]{1,0:T(8,128)(2,1)S(1)} custom-call(bf16[16,2,4,32,256]{4,3,2,1,0:T(8,128)(2,1)} %all-to-all-done.refs_0_, bf16[1024,1024]{1,0:T(8,128)(2,1)S(1)} %copy-done.1, bf16[12,512,256]{2,1,0:T(8,128)(2,1)S(1)} %bitcast.14), custom_call_target="tpu_custom_call" | custom-call | flops 2147483648 | bytes 4194304 | tf_op jit(solution)/shard_map/to_columns/pallas_call | solution.py:241
  44.3 0.0 copy-start
  44.4 1.3 copy-done
  45.7 10.2 %all-to-all-start.1 = ((bf16[128,8,1024]{2,1,0:T(8,128)(2,1)}), bf16[128,8,1024]{2,1,0:T(8,128)(2,1)}, u32[]{:S(2)}, u32[]{:S(2)}) async-start(bf16[128,8,1024]{2,1,0:T(8,128)(2,1)} %bitcast.16), calls=%async_computation.1 | async-start | bytes 4194304 | tf_op jit(solution)/shard_map/all_to_all | solution.py:250
  55.9 30.4 %all-to-all-done.1 = bf16[128,8,1024]{2,1,0:T(8,128)(2,1)} async-done(((bf16[128,8,1024]{2,1,0:T(8,128)(2,1)}), bf16[128,8,1024]{2,1,0:T(8,128)(2,1)}, u32[]{:S(2)}, u32[]{:S(2)}) %all-to-all-start.1) | async-done | bytes 2097184 | tf_op jit(solution)/shard_map/all_to_all | solution.py:250
  86.2 0.0 copy-start.3
  86.2 1.6 copy-done.3
  87.8 0.0 copy-start.4
  87.8 1.6 copy-done.4
  89.4 25.0 %on_sites.1 = bf16[1024,1024]{1,0:T(8,128)(2,1)S(1)} custom-call(s32[1]{0:T(128)} %bitcast.refs_0_, bf16[1024,1024]{1,0:T(8,128)(2,1)} %bitcast.6.refs_1_, bf16[1024,1024]{1,0:T(8,128)(2,1)S(1)} %copy-done.4, bf16[12,512,256]{2,1,0:T(8,128)(2,1)S(1)} %bitcast.15, bf16[1024,1024]{1,0:T(8,128)(2,1)S(1)} %copy-done.3), custom_call_target="tpu_custom_call" | custom-call | flops 17179869184 | bytes 4194304 | tf_op jit(solution)/shard_map/on_sites/pallas_call | solution.py:252
  114.5 0.0 copy-start.2
  114.5 34.9 %all_to_all.32 = bf16[128,8,1024]{2,1,0:T(8,128)(2,1)S(1)} all-to-all(bf16[128,8,1024]{2,1,0:T(8,128)(2,1)S(1)} %bitcast.17), channel_id=1, replica_groups=mesh['kx'=8,'ky'=16] {'kx','ky'}, dimensions={0} | all-to-all | bytes 4194304 | tf_op jit(solution)/shard_map/all_to_all | solution.py:270
  149.4 0.0 copy-done.2
  149.4 4.0 %to_rows.1 = bf16[16,2,4,32,256]{4,3,2,1,0:T(8,128)(2,1)S(1)} custom-call(bf16[1024,1024]{1,0:T(8,128)(2,1)S(1)} %bitcast.18, bf16[1024,1024]{1,0:T(8,128)(2,1)S(1)} %copy-done.2), custom_call_target="tpu_custom_call" | custom-call | flops 2147483648 | bytes 4194304 | tf_op jit(solution)/shard_map/to_rows/pallas_call | solution.py:271
  153.4 30.1 %all_to_all.33 = bf16[16,2,4,32,256]{4,3,2,1,0:T(8,128)(2,1)S(1)} all-to-all(bf16[16,2,4,32,256]{4,3,2,1,0:T(8,128)(2,1)S(1)} %to_rows.1), channel_id=1, replica_groups=mesh['kx'=8,'ky'=16] {'ky'}, dimensions={0} | all-to-all | bytes 4194304 | tf_op jit(solution)/shard_map/all_to_all | solution.py:280
  183.5 0.5 convert_bitcast_fusion
  184.0 2.3 %copy.10 = f32[2,16,4,32,256]{4,3,2,1,0:T(8,128)} copy(f32[2,16,4,32,256]{4,3,2,0,1:T(8,128)S(1)} %convert_bitcast_fusion) | data formatting | bytes 8388608 | tf_op jit(solution)/shard_map/convert_element_type | solution.py:281
Async XLA Ops:
  3.2 34.5 %all-to-all-start = ((bf16[16,2,4,32,256]{4,3,2,1,0:T(8,128)(2,1)}), bf16[16,2,4,32,256]{4,3,2,1,0:T(8,128)(2,1)}, u32[]{:S(2)}, u32[]{:S(2)}) async-start(bf16[16,2,4,32,256]{4,3,2,1,0:T(8,128)(2,1)} %bitcast.13), calls=%async_computation | async-start | bytes 4194304 | tf_op jit(solution)/shard_map/all_to_all | solution.py:240
  37.7 1.6 copy-start.1
  44.3 1.3 copy-start
  45.7 40.6 %all-to-all-start.1 = ((bf16[128,8,1024]{2,1,0:T(8,128)(2,1)}), bf16[128,8,1024]{2,1,0:T(8,128)(2,1)}, u32[]{:S(2)}, u32[]{:S(2)}) async-start(bf16[128,8,1024]{2,1,0:T(8,128)(2,1)} %bitcast.16), calls=%async_computation.1 | async-start | bytes 4194304 | tf_op jit(solution)/shard_map/all_to_all | solution.py:250
  86.2 1.6 copy-start.3
  87.8 1.6 copy-start.4
  114.5 35.0 %copy-start.2 = (bf16[1024,1024]{1,0:T(8,128)(2,1)S(1)}, bf16[1024,1024]{1,0:T(8,128)(2,1)}, u32[]{:S(2)}) copy-start(bf16[1024,1024]{1,0:T(8,128)(2,1)} %constant.22.clone.refs_1_) | copy-start | bytes 6291460

commit v3 on v2

--- a/solution.py
+++ b/solution.py
@@ -46,22 +46,25 @@
     b_x = b_x.transpose(1, 0, 2, 3).reshape(n, n)
     b_y = complex_table(natural, own.T.reshape(-1), length, -1.0, 1.0 / length)
     b_y = b_y.reshape(2, length, 2, quad, groups).transpose(0, 1, 3, 2, 4).reshape(n, n)
-    return [t.astype(ml_dtypes.bfloat16) for t in (t_y, t_x, b_x, b_y)]
+    return np.stack([t_y, t_x, b_x, b_y]).astype(ml_dtypes.bfloat16)
 
 
 def dot(left, right):
     return jnp.dot(left, right, preferred_element_type=jnp.float32)
 
 
-def columns_kernel(quad, groups, freqs, block_ref, table_ref, panel_hbm, out_ref, wide_ref):
-    del panel_hbm
+def dot_turned(left, right):
+    return lax.dot_general(left, right, (((1,), (1,)), ((), ())), preferred_element_type=jnp.float32)
+
+
+def columns_kernel(quad, groups, freqs, block_ref, table_ref, out_ref, wide_ref):
     length = quad * groups
 
     def row(r, carry):
         rhs = jnp.concatenate(
             [block_ref[:, c, r].reshape(length, freqs) for c in range(2)], 0
         )
-        product = dot(table_ref[...], rhs)
+        product = dot(table_ref[0], rhs)
         for col in range(quad):
             for c in range(2):
                 m = (col * 2 + c) * groups
@@ -96,32 +99,17 @@
     ref[col, 2 * c + 1, :TILE, :] = jnp.where(top, low, high)
 
 
-def sites_kernel(
-    quad, freqs, bosons, spot_ref, block_ref, fore_hbm, panel_hbm, back_hbm, out_ref,
-    fore_ref, panel_ref, back_ref, green_ref, field_ref, fore_sem, panel_sem, back_sem,
-):
+def sites_kernel(quad, freqs, bosons, block_ref, table_ref, vertex_ref, out_ref, green_ref, field_ref):
     half = green_ref.shape[2]
-    first = spot_ref[0] == 0
-    fore = [
-        pltpu.make_async_copy(fore_hbm.at[pl.ds(i * half, half)], fore_ref.at[pl.ds(i * half, half)], fore_sem.at[i])
-        for i in range(4)
-    ]
-    for copy in fore:
-        copy.start()
-    panel = pltpu.make_async_copy(panel_hbm, panel_ref, panel_sem)
-    panel.start()
-    back = pltpu.make_async_copy(back_hbm, back_ref, back_sem)
-    back.start()
+    first = lax.axis_index("kx") + lax.axis_index("ky") == 0
 
     for i in range(4):
-        fore[i].wait()
-        lattice = dot(fore_ref[i * half : (i + 1) * half, :], block_ref[...]).astype(jnp.bfloat16)
+        lattice = dot(table_ref[1, i * half : (i + 1) * half, :], block_ref[...]).astype(jnp.bfloat16)
         for col in range(quad):
             green_ref[col, i] = lattice[:, col * freqs : (col + 1) * freqs]
     for col in range(quad // 2, quad):
         for c in range(2):
             swap_first(green_ref, col, c)
-    panel.wait()
 
     def pair_block(step, carry):
         column, side = step // 2, step % 2
@@ -140,18 +128,19 @@
         for start in range(0, bosons, GROUP):
             sums = None
             for w in range(start, min(start + GROUP, bosons)):
+                panel = jnp.concatenate([vertex_ref[0, w], vertex_ref[1, w]], 1)
                 sp_re, sp_im = shifted(p_re, w), shifted(p_im, w)
                 sq_re, sq_im = shifted(q_re, w), shifted(q_im, w)
-                lefts = []
+                cross = []
                 for g_re, g_im, m_re, m_im in (
                     (p_re, p_im, mirror(sp_re, sq_re), mirror(sp_im, sq_im)),
                     (q_re, q_im, mirror(sq_re, sp_re), mirror(sq_im, sp_im)),
                 ):
                     b_re = g_re * m_re - g_im * m_im
                     b_im = g_re * m_im + g_im * m_re
-                    lefts += [jnp.concatenate([b_re, -b_im], 1), jnp.concatenate([b_im, b_re], 1)]
-                cross = dot(jnp.concatenate(lefts, 0), panel_ref[w]).astype(jnp.bfloat16)
-                cp_re, cp_im, cq_re, cq_im = [cross[i * half : (i + 1) * half] for i in range(4)]
+                    for left in (jnp.concatenate([b_re, -b_im], 1), jnp.concatenate([b_im, b_re], 1)):
+                        cross.append(dot_turned(left, panel).astype(jnp.bfloat16))
+                cp_re, cp_im, cq_re, cq_im = cross
                 terms = [
                     sp_re * cp_re - sp_im * cp_im,
                     sp_re * cp_im + sp_im * cp_re,
@@ -172,10 +161,9 @@
     for col in range(quad // 2, quad):
         for c in range(2):
             swap_first(field_ref, col, c)
-    back.wait()
     for col in range(quad):
         stacked = field_ref[col].reshape(4 * half, freqs)
-        out_ref[:, col * freqs : (col + 1) * freqs] = dot(back_ref[...], stacked).astype(jnp.bfloat16)
+        out_ref[:, col * freqs : (col + 1) * freqs] = dot(table_ref[2], stacked).astype(jnp.bfloat16)
 
 
 def rows_kernel(quad, groups, freqs, block_ref, table_ref, out_ref, wide_ref, rhs_ref):
@@ -197,7 +185,7 @@
                 for k in range(freqs // LANES):
                     part = wide_ref[col * (freqs // LANES) + k, pl.ds(r * 2 + c, groups, stride=2 * quad), :]
                     rhs_ref[m : m + groups, k * LANES : (k + 1) * LANES] = part.astype(jnp.bfloat16)
-        product = dot(table_ref[...], rhs_ref[...]).astype(jnp.bfloat16)
+        product = dot(table_ref[3], rhs_ref[...]).astype(jnp.bfloat16)
         for c in range(2):
             part = product[c * length : (c + 1) * length]
             out_ref[:, c, r] = part.reshape(targets, width, freqs)
@@ -231,42 +219,30 @@
     quad = length // groups
     bosons = vertex.shape[1]
     n = 2 * length
-    t_y, t_x, b_x, b_y = [jnp.asarray(t) for t in tables(length, groups)]
+    dfts = jnp.asarray(tables(length, groups))
     both = ("kx", "ky")
-
-    panels = vertex.transpose(1, 0, 3, 2).reshape(bosons, 2 * freqs, freqs)
 
     block = green.reshape(2, ky, quad, width, freqs).transpose(1, 0, 2, 3, 4)
     block = lax.all_to_all(block, "ky", split_axis=0, concat_axis=0, tiled=True)
     spectrum = call(
         lambda *refs: columns_kernel(quad, groups, freqs, *refs),
         (n, quad * freqs),
-        [in_vmem()] * 2 + [pl.BlockSpec(memory_space=pltpu.HBM)],
+        [in_vmem()] * 2,
         [pltpu.VMEM((quad * freqs // LANES, n, LANES), jnp.float32)],
         2 * n * n * quad * freqs,
         16,
         "to_columns",
-    )(block, t_y, panels)
+    )(block, dfts)
     spectrum = lax.all_to_all(spectrum, both, split_axis=0, concat_axis=0, tiled=True)
-    spot = (lax.axis_index("kx") * ky + lax.axis_index("ky")).astype(jnp.int32).reshape(1)
     field = call(
         lambda *refs: sites_kernel(quad, freqs, bosons, *refs),
         (n, quad * freqs),
-        [pl.BlockSpec(memory_space=pltpu.SMEM), in_vmem()] + [pl.BlockSpec(memory_space=pltpu.HBM)] * 3,
-        [
-            pltpu.VMEM((n, n), jnp.bfloat16),
-            pltpu.VMEM((bosons, 2 * freqs, freqs), jnp.bfloat16),
-            pltpu.VMEM((n, n), jnp.bfloat16),
-            pltpu.VMEM((quad, 4, length // 2, freqs), jnp.bfloat16),
-            pltpu.VMEM((quad, 4, length // 2, freqs), jnp.bfloat16),
-            pltpu.SemaphoreType.DMA((4,)),
-            pltpu.SemaphoreType.DMA,
-            pltpu.SemaphoreType.DMA,
-        ],
+        [in_vmem()] * 3,
+        [pltpu.VMEM((quad, 4, length // 2, freqs), jnp.bfloat16)] * 2,
         2 * n * n * quad * freqs * 2 + 8 * bosons * length * quad * freqs * freqs,
-        36,
+        24,
         "on_sites",
-    )(spot, spectrum, t_x, panels, b_x)
+    )(spectrum, dfts, vertex)
     field = lax.all_to_all(field, both, split_axis=0, concat_axis=0, tiled=True)
     settled = call(
         lambda *refs: rows_kernel(quad, groups, freqs, *refs),
@@ -276,7 +252,7 @@
         2 * n * n * quad * freqs,
         16,
         "to_rows",
-    )(field, b_y)
+    )(field, dfts)
     settled = lax.all_to_all(settled, "ky", split_axis=0, concat_axis=0, tiled=True)
     return settled.transpose(1, 0, 2, 3, 4).reshape(2, rows, width, freqs).astype(jnp.float32)
 

time: 187 us -> 170 us (0.909)
  blocking collectives: 65 us -> 138 us
  waiting for transfers between devices: 54.9 us -> 0 us
  starting transfers between devices: 17 us -> 0 us
  local copies, waits for them, and re-layouts: 14.8 us -> 4.26 us
  Pallas kernels: 34.1 us -> 27.3 us
    all_to_all x0 -> x2, blocking collectives: none -> 72.5 us  [the longest x1 38.8 us: per_device(): lax.all_to_all(spectrum, both, split_axis=0, concat_axis=0, tiled=True)]
    all_to_all x2 -> x0, waiting for transfers between devices: 54.9 us -> none  [the longest x1 30.4 us: per_device(): lax.all_to_all(spectrum, both, split_axis=0, concat_axis=0, tiled=True)]
    all_to_all x2 -> x0, starting transfers between devices: 17 us -> none  [the longest x1 10.2 us: per_device(): lax.all_to_all(spectrum, both, split_axis=0, concat_axis=0, tiled=True)]
    unnamed x10 -> x4, local copies, waits for them, and re-layouts: 6.09 us -> 0.01 us
    pallas_call x1, Pallas kernels: 25 us -> 19.9 us  [per_device(): call(lambda *refs: sites_kernel(quad, freqs, bosons, *refs), (n, quad * f...]
    transpose x1 -> x0, local copies, waits for them, and re-layouts: 3.19 us -> none  [per_device(): panels = vertex.transpose(1, 0, 3, 2).reshape(bosons, 2 * freqs, freqs)]
  transfers between devices with their start and end apart: 2 -> 0, of which waited for: 2 -> 0; matrix products, arithmetic and copies ran while one was open for 2% -> 0% of each run, Pallas kernels for 0% -> 0%
where the time goes in v3:
time: 170 us
  blocking collectives  138 us (81%)
  Pallas kernels  27.3 us (16%)
  local copies, waits for them, and re-layouts  4.26 us (3%)
    all_to_all x1, blocking collectives, per_device(): lax.all_to_all(spectrum, both, split_axis=0, concat_axis=0, tiled=True)  38.8 us
    all_to_all x1, blocking collectives, per_device(): field = lax.all_to_all(field, both, split_axis=0, concat_axis=0, tiled=True)  34.9 us
    all_to_all x1, blocking collectives, per_device(): block = lax.all_to_all(block, 'ky', split_axis=0, concat_axis=0, tiled=True)  33.6 us
    all_to_all x1, blocking collectives, per_device(): lax.all_to_all(settled, 'ky', split_axis=0, concat_axis=0, tiled=True)  30.1 us
    pallas_call x1, Pallas kernels, per_device(): call(lambda *refs: sites_kernel(quad, freqs, bosons, *refs), (n, quad * f...  19.9 us
    pallas_call x1, Pallas kernels, per_device(): call(lambda *refs: rows_kernel(quad, groups, freqs, *refs), (ky, 2, quad,...  4 us
    pallas_call x1, Pallas kernels, per_device(): call(lambda *refs: columns_kernel(quad, groups, freqs, *refs), (n, quad *...  3.46 us

profile of v3, /device:TPU:1, one launch (start us, length us, event | category | flops | bytes accessed | tf_op | source)
XLA Modules:
  0.0 169.7 jit_solution(18346147848539078409)
XLA Ops:
  0.0 0.0 copy-start
  0.0 1.9 %copy.7 = bf16[2,16,4,32,256]{4,3,2,0,1:T(8,128)(2,1)S(1)} copy(bf16[2,16,4,32,256]{4,3,2,1,0:T(8,128)(2,1)} %bitcast.16) | data formatting | bytes 4194304 | tf_op jit(solution)/shard_map/reshape | solution.py:225
  1.9 33.6 %all_to_all.32.refs_0_ = bf16[16,2,4,32,256]{4,3,2,1,0:T(8,128)(2,1)S(1)} all-to-all(bf16[16,2,4,32,256]{4,3,2,1,0:T(8,128)(2,1)S(1)} %bitcast.15), channel_id=1, replica_groups=mesh['kx'=8,'ky'=16] {'ky'}, dimensions={0} | all-to-all | bytes 4194304 | tf_op jit(solution)/shard_map/all_to_all | solution.py:226
  35.5 0.0 copy-done
  35.6 3.5 %to_columns.1 = bf16[1024,1024]{1,0:T(8,128)(2,1)S(1)} custom-call(bf16[16,2,4,32,256]{4,3,2,1,0:T(8,128)(2,1)S(1)} %all_to_all.32.refs_0_, bf16[4,1024,1024]{2,1,0:T(8,128)(2,1)S(1)} %copy-done), custom_call_target="tpu_custom_call" | custom-call | flops 2147483648 | bytes 4194304 | tf_op jit(solution)/shard_map/to_columns/pallas_call | solution.py:227
  39.0 0.0 copy-start.1
  39.0 38.8 %all_to_all.33 = bf16[128,8,1024]{2,1,0:T(8,128)(2,1)S(1)} all-to-all(bf16[128,8,1024]{2,1,0:T(8,128)(2,1)S(1)} %bitcast.12), channel_id=1, replica_groups=mesh['kx'=8,'ky'=16] {'kx','ky'}, dimensions={0} | all-to-all | bytes 4194304 | tf_op jit(solution)/shard_map/all_to_all | solution.py:236
  77.9 0.0 copy-done.1
  77.9 19.9 %on_sites.1 = bf16[1024,1024]{1,0:T(8,128)(2,1)S(1)} custom-call(bf16[1024,1024]{1,0:T(8,128)(2,1)S(1)} %bitcast.13, bf16[4,1024,1024]{2,1,0:T(8,128)(2,1)S(1)} %copy-done, bf16[2,12,256,256]{3,2,1,0:T(8,128)(2,1)S(1)} %copy-done.1), custom_call_target="tpu_custom_call" | custom-call | flops 17179869184 | bytes 4194304 | tf_op jit(solution)/shard_map/on_sites/pallas_call | solution.py:237
  97.7 34.9 %all_to_all.34 = bf16[128,8,1024]{2,1,0:T(8,128)(2,1)S(1)} all-to-all(bf16[128,8,1024]{2,1,0:T(8,128)(2,1)S(1)} %bitcast.14), channel_id=1, replica_groups=mesh['kx'=8,'ky'=16] {'kx','ky'}, dimensions={0} | all-to-all | bytes 4194304 | tf_op jit(solution)/shard_map/all_to_all | solution.py:246
  132.7 4.0 %to_rows.1 = bf16[16,2,4,32,256]{4,3,2,1,0:T(8,128)(2,1)S(1)} custom-call(bf16[1024,1024]{1,0:T(8,128)(2,1)S(1)} %bitcast.11, bf16[4,1024,1024]{2,1,0:T(8,128)(2,1)S(1)} %copy-done), custom_call_target="tpu_custom_call" | custom-call | flops 2147483648 | bytes 4194304 | tf_op jit(solution)/shard_map/to_rows/pallas_call | solution.py:247
  136.7 30.1 %all_to_all.35 = bf16[16,2,4,32,256]{4,3,2,1,0:T(8,128)(2,1)S(1)} all-to-all(bf16[16,2,4,32,256]{4,3,2,1,0:T(8,128)(2,1)S(1)} %to_rows.1), channel_id=1, replica_groups=mesh['kx'=8,'ky'=16] {'ky'}, dimensions={0} | all-to-all | bytes 4194304 | tf_op jit(solution)/shard_map/all_to_all | solution.py:256
  166.8 0.5 convert_bitcast_fusion
  167.3 2.3 %copy.5 = f32[2,16,4,32,256]{4,3,2,1,0:T(8,128)} copy(f32[2,16,4,32,256]{4,3,2,0,1:T(8,128)S(1)} %convert_bitcast_fusion) | data formatting | bytes 8388608 | tf_op jit(solution)/shard_map/convert_element_type | solution.py:257
Async XLA Ops:
  0.0 35.5 %copy-start = (bf16[4,1024,1024]{2,1,0:T(8,128)(2,1)S(1)}, bf16[4,1024,1024]{2,1,0:T(8,128)(2,1)}, u32[]{:S(2)}) copy-start(bf16[4,1024,1024]{2,1,0:T(8,128)(2,1)} %constant.2.clone.refs_1_) | copy-start | bytes 25165828
  39.0 38.8 %copy-start.1 = (bf16[2,12,256,256]{3,2,1,0:T(8,128)(2,1)S(1)}, bf16[2,12,256,256]{3,2,1,0:T(8,128)(2,1)}, u32[]{:S(2)}) copy-start(bf16[2,12,256,256]{3,2,1,0:T(8,128)(2,1)} %refs_2_.1) | copy-start | bytes 9437188

commit v4 on v3

--- a/solution.py
+++ b/solution.py
@@ -31,22 +31,23 @@
 
 def tables(length, groups):
     quad = length // groups
-    half_quad = quad // 2
+    half = length // 2
     pairs = pair_list(length)
-    natural = np.arange(length)
-    own = np.stack(
-        [pairs[: length // 2].reshape(groups, half_quad), pairs[length // 2 :].reshape(groups, half_quad)], 1
-    ).reshape(groups, quad)
-    n = 2 * length
-    t_y = complex_table(own.T.reshape(-1), natural, length, 1.0, 1.0)
-    t_y = t_y.reshape(2, quad, groups, 2, length).transpose(1, 0, 2, 3, 4).reshape(n, n)
-    t_x = complex_table(pairs, natural, length, 1.0, 1.0 / length)
-    t_x = t_x.reshape(2, length, 2, length).transpose(0, 1, 3, 2).reshape(n, n)
-    b_x = complex_table(natural, pairs, length, -1.0, 1.0)
-    b_x = b_x.transpose(1, 0, 2, 3).reshape(n, n)
-    b_y = complex_table(natural, own.T.reshape(-1), length, -1.0, 1.0 / length)
-    b_y = b_y.reshape(2, length, 2, quad, groups).transpose(0, 1, 3, 2, 4).reshape(n, n)
-    return np.stack([t_y, t_x, b_x, b_y]).astype(ml_dtypes.bfloat16)
+    low = np.arange(half)
+    own = np.stack([pairs[:half].reshape(groups, -1), pairs[half:].reshape(groups, -1)], 1).reshape(groups, quad)
+    found = []
+    for parity in range(2):
+        y = own[:, parity::2].T.reshape(-1)
+        x = np.concatenate([pairs[:half][parity::2], pairs[half:][parity::2]])
+        cols = quad // 2
+        t_y = complex_table(y, low, length, 1.0, 1.0)
+        t_y = t_y.reshape(2, cols, groups, 2, half).transpose(1, 0, 2, 3, 4)
+        t_x = complex_table(x, low, length, 1.0, 1.0 / length).transpose(0, 1, 3, 2)
+        b_x = complex_table(low, x, length, -1.0, 1.0).transpose(1, 0, 2, 3)
+        b_y = complex_table(low, y, length, -1.0, 1.0 / length)
+        b_y = b_y.reshape(2, half, 2, cols, groups).transpose(0, 1, 3, 2, 4)
+        found.append([t.reshape(length, length) for t in (t_y, t_x, b_x, b_y)])
+    return np.stack([np.stack(f) for f in found], 1).astype(ml_dtypes.bfloat16)
 
 
 def dot(left, right):
@@ -61,14 +62,14 @@
     length = quad * groups
 
     def row(r, carry):
-        rhs = jnp.concatenate(
-            [block_ref[:, c, r].reshape(length, freqs) for c in range(2)], 0
-        )
-        product = dot(table_ref[0], rhs)
-        for col in range(quad):
-            for c in range(2):
-                m = (col * 2 + c) * groups
-                part = product[m : m + groups]
+        both = [block_ref[:, c, r].reshape(length, freqs) for c in range(2)]
+        low, high = [b[: length // 2] for b in both], [b[length // 2 :] for b in both]
+        for parity in range(2):
+            rhs = jnp.concatenate([a - b if parity else a + b for a, b in zip(low, high)], 0)
+            product = dot(table_ref[0, parity], rhs)
+            for at in range(quad):
+                col, c = 2 * (at // 2) + parity, at % 2
+                part = product[at * groups : (at + 1) * groups]
                 for k in range(freqs // LANES):
                     spots = pl.ds(r * 2 + c, groups, stride=2 * quad)
                     wide_ref[col * (freqs // LANES) + k, spots, :] = part[:, k * LANES : (k + 1) * LANES]
@@ -99,17 +100,27 @@
     ref[col, 2 * c + 1, :TILE, :] = jnp.where(top, low, high)
 
 
-def sites_kernel(quad, freqs, bosons, block_ref, table_ref, vertex_ref, out_ref, green_ref, field_ref):
+def sites_kernel(quad, freqs, bosons, block_ref, table_ref, vertex_ref, out_ref, green_ref, field_ref, mixed_ref):
     half = green_ref.shape[2]
+    length = 2 * half
+    part = half // 2
     first = lax.axis_index("kx") + lax.axis_index("ky") == 0
 
-    for i in range(4):
-        lattice = dot(table_ref[1, i * half : (i + 1) * half, :], block_ref[...]).astype(jnp.bfloat16)
-        for col in range(quad):
-            green_ref[col, i] = lattice[:, col * freqs : (col + 1) * freqs]
+    low, high = block_ref[:length, :], block_ref[length:, :]
+    for parity in range(2):
+        lattice = dot(table_ref[1, parity], low - high if parity else low + high).astype(jnp.bfloat16)
+        for at in range(4):
+            for col in range(quad):
+                green_ref[col, at, parity * part : (parity + 1) * part, :] = lattice[
+                    at * part : (at + 1) * part, col * freqs : (col + 1) * freqs
+                ]
     for col in range(quad // 2, quad):
         for c in range(2):
             swap_first(green_ref, col, c)
+    for w in range(bosons):
+        v_re, v_im = vertex_ref[0, w], vertex_ref[1, w]
+        mixed_ref[0, w] = v_im - v_re
+        mixed_ref[1, w] = v_re + v_im
 
     def pair_block(step, carry):
         column, side = step // 2, step % 2
@@ -128,19 +139,20 @@
         for start in range(0, bosons, GROUP):
             sums = None
             for w in range(start, min(start + GROUP, bosons)):
-                panel = jnp.concatenate([vertex_ref[0, w], vertex_ref[1, w]], 1)
                 sp_re, sp_im = shifted(p_re, w), shifted(p_im, w)
                 sq_re, sq_im = shifted(q_re, w), shifted(q_im, w)
-                cross = []
+                b_re, b_im = [], []
                 for g_re, g_im, m_re, m_im in (
                     (p_re, p_im, mirror(sp_re, sq_re), mirror(sp_im, sq_im)),
                     (q_re, q_im, mirror(sq_re, sp_re), mirror(sq_im, sp_im)),
                 ):
-                    b_re = g_re * m_re - g_im * m_im
-                    b_im = g_re * m_im + g_im * m_re
-                    for left in (jnp.concatenate([b_re, -b_im], 1), jnp.concatenate([b_im, b_re], 1)):
-                        cross.append(dot_turned(left, panel).astype(jnp.bfloat16))
-                cp_re, cp_im, cq_re, cq_im = cross
+                    b_re.append(g_re * m_re - g_im * m_im)
+                    b_im.append(g_re * m_im + g_im * m_re)
+                b_re, b_im = jnp.concatenate(b_re, 0), jnp.concatenate(b_im, 0)
+                shared = dot_turned(b_re + b_im, vertex_ref[0, w])
+                c_re = (shared - dot_turned(b_im, mixed_ref[1, w])).astype(jnp.bfloat16)
+                c_im = (shared + dot_turned(b_re, mixed_ref[0, w])).astype(jnp.bfloat16)
+                cp_re, cq_re, cp_im, cq_im = c_re[:half], c_re[half:], c_im[:half], c_im[half:]
                 terms = [
                     sp_re * cp_re - sp_im * cp_im,
                     sp_re * cp_im + sp_im * cp_re,
@@ -162,8 +174,16 @@
         for c in range(2):
             swap_first(field_ref, col, c)
     for col in range(quad):
-        stacked = field_ref[col].reshape(4 * half, freqs)
-        out_ref[:, col * freqs : (col + 1) * freqs] = dot(table_ref[2], stacked).astype(jnp.bfloat16)
+        lanes = slice(col * freqs, (col + 1) * freqs)
+        even, odd = [
+            dot(
+                table_ref[2, parity],
+                field_ref[col, :, parity * part : (parity + 1) * part, :].reshape(length, freqs),
+            )
+            for parity in range(2)
+        ]
+        out_ref[:length, lanes] = (even + odd).astype(jnp.bfloat16)
+        out_ref[length:, lanes] = (even - odd).astype(jnp.bfloat16)
 
 
 def rows_kernel(quad, groups, freqs, block_ref, table_ref, out_ref, wide_ref, rhs_ref):
@@ -181,14 +201,20 @@
     def row(r, carry):
         for col in range(quad):
             for c in range(2):
-                m = (col * 2 + c) * groups
+                m = (col % 2) * length + ((col // 2) * 2 + c) * groups
                 for k in range(freqs // LANES):
                     part = wide_ref[col * (freqs // LANES) + k, pl.ds(r * 2 + c, groups, stride=2 * quad), :]
                     rhs_ref[m : m + groups, k * LANES : (k + 1) * LANES] = part.astype(jnp.bfloat16)
-        product = dot(table_ref[3], rhs_ref[...]).astype(jnp.bfloat16)
-        for c in range(2):
-            part = product[c * length : (c + 1) * length]
-            out_ref[:, c, r] = part.reshape(targets, width, freqs)
+        even, odd = [
+            dot(table_ref[3, parity], rhs_ref[parity * length : (parity + 1) * length, :]) for parity in range(2)
+        ]
+        for upper, total in ((0, even + odd), (1, even - odd)):
+            total = total.astype(jnp.bfloat16)
+            for c in range(2):
+                part = total[c * (length // 2) : (c + 1) * (length // 2)]
+                out_ref[upper * (targets // 2) : (upper + 1) * (targets // 2), c, r] = part.reshape(
+                    targets // 2, width, freqs
+                )
         return carry
 
     lax.fori_loop(0, quad, row, 0)
@@ -229,7 +255,7 @@
         (n, quad * freqs),
         [in_vmem()] * 2,
         [pltpu.VMEM((quad * freqs // LANES, n, LANES), jnp.float32)],
-        2 * n * n * quad * freqs,
+        n * n * quad * freqs,
         16,
         "to_columns",
     )(block, dfts)
@@ -238,8 +264,9 @@
         lambda *refs: sites_kernel(quad, freqs, bosons, *refs),
         (n, quad * freqs),
         [in_vmem()] * 3,
-        [pltpu.VMEM((quad, 4, length // 2, freqs), jnp.bfloat16)] * 2,
-        2 * n * n * quad * freqs * 2 + 8 * bosons * length * quad * freqs * freqs,
+        [pltpu.VMEM((quad, 4, length // 2, freqs), jnp.bfloat16)] * 2
+        + [pltpu.VMEM((2, bosons, freqs, freqs), jnp.bfloat16)],
+        2 * n * n * quad * freqs + 6 * bosons * length * quad * freqs * freqs,
         24,
         "on_sites",
     )(spectrum, dfts, vertex)
@@ -249,7 +276,7 @@
         (ky, 2, quad, width, freqs),
         [in_vmem()] * 2,
         [pltpu.VMEM((quad * freqs // LANES, n, LANES), jnp.float32), pltpu.VMEM((n, freqs), jnp.bfloat16)],
-        2 * n * n * quad * freqs,
+        n * n * quad * freqs,
         16,
         "to_rows",
     )(field, dfts)

time: 170 us -> 166 us (0.976)
  Pallas kernels: 27.3 us -> 23.5 us
    pallas_call x1, Pallas kernels: 19.9 us -> 17.7 us  [per_device(): call(lambda *refs: sites_kernel(quad, freqs, bosons, *refs), (n, quad * f...]
where the time goes in v4:
time: 166 us
  blocking collectives  138 us (83%)
  Pallas kernels  23.5 us (14%)
  local copies, waits for them, and re-layouts  4.11 us (2%)
    all_to_all x1, blocking collectives, per_device(): lax.all_to_all(spectrum, both, split_axis=0, concat_axis=0, tiled=True)  38.8 us
    all_to_all x1, blocking collectives, per_device(): field = lax.all_to_all(field, both, split_axis=0, concat_axis=0, tiled=True)  34.9 us
    all_to_all x1, blocking collectives, per_device(): block = lax.all_to_all(block, 'ky', split_axis=0, concat_axis=0, tiled=True)  33.6 us
    all_to_all x1, blocking collectives, per_device(): lax.all_to_all(settled, 'ky', split_axis=0, concat_axis=0, tiled=True)  30.1 us
    pallas_call x1, Pallas kernels, per_device(): call(lambda *refs: sites_kernel(quad, freqs, bosons, *refs), (n, quad * f...  17.7 us

profile of v4, /device:TPU:1, one launch (start us, length us, event | category | flops | bytes accessed | tf_op | source)
XLA Modules:
  0.0 165.7 jit_solution(16743770616681190270)
XLA Ops:
  0.0 1.8 %copy.7 = bf16[2,16,4,32,256]{4,3,2,0,1:T(8,128)(2,1)S(1)} copy(bf16[2,16,4,32,256]{4,3,2,1,0:T(8,128)(2,1)} %bitcast.16) | data formatting | bytes 4194304 | tf_op jit(solution)/shard_map/reshape | solution.py:251
  1.8 0.0 copy-start
  1.8 33.6 %all_to_all.32.refs_0_ = bf16[16,2,4,32,256]{4,3,2,1,0:T(8,128)(2,1)S(1)} all-to-all(bf16[16,2,4,32,256]{4,3,2,1,0:T(8,128)(2,1)S(1)} %bitcast.15), channel_id=1, replica_groups=mesh['kx'=8,'ky'=16] {'ky'}, dimensions={0} | all-to-all | bytes 4194304 | tf_op jit(solution)/shard_map/all_to_all | solution.py:252
  35.4 0.0 copy-done
  35.4 2.7 %to_columns.1 = bf16[1024,1024]{1,0:T(8,128)(2,1)S(1)} custom-call(bf16[16,2,4,32,256]{4,3,2,1,0:T(8,128)(2,1)S(1)} %all_to_all.32.refs_0_, bf16[4,2,512,512]{3,2,1,0:T(8,128)(2,1)S(1)} %copy-done), custom_call_target="tpu_custom_call" | custom-call | flops 1073741824 | bytes 4194304 | tf_op jit(solution)/shard_map/to_columns/pallas_call | solution.py:253
  38.1 0.0 copy-start.1
  38.1 38.8 %all_to_all.33 = bf16[128,8,1024]{2,1,0:T(8,128)(2,1)S(1)} all-to-all(bf16[128,8,1024]{2,1,0:T(8,128)(2,1)S(1)} %bitcast.12), channel_id=1, replica_groups=mesh['kx'=8,'ky'=16] {'kx','ky'}, dimensions={0} | all-to-all | bytes 4194304 | tf_op jit(solution)/shard_map/all_to_all | solution.py:262
  77.0 0.0 copy-done.1
  77.0 17.7 %on_sites.1 = bf16[1024,1024]{1,0:T(8,128)(2,1)S(1)} custom-call(bf16[1024,1024]{1,0:T(8,128)(2,1)S(1)} %bitcast.13, bf16[4,2,512,512]{3,2,1,0:T(8,128)(2,1)S(1)} %copy-done, bf16[2,12,256,256]{3,2,1,0:T(8,128)(2,1)S(1)} %copy-done.1), custom_call_target="tpu_custom_call" | custom-call | flops 11811160064 | bytes 4194304 | tf_op jit(solution)/shard_map/on_sites/pallas_call | solution.py:263
  94.7 34.9 %all_to_all.34 = bf16[128,8,1024]{2,1,0:T(8,128)(2,1)S(1)} all-to-all(bf16[128,8,1024]{2,1,0:T(8,128)(2,1)S(1)} %bitcast.14), channel_id=1, replica_groups=mesh['kx'=8,'ky'=16] {'kx','ky'}, dimensions={0} | all-to-all | bytes 4194304 | tf_op jit(solution)/shard_map/all_to_all | solution.py:273
  129.7 3.0 %to_rows.1 = bf16[16,2,4,32,256]{4,3,2,1,0:T(8,128)(2,1)S(1)} custom-call(bf16[1024,1024]{1,0:T(8,128)(2,1)S(1)} %bitcast.11, bf16[4,2,512,512]{3,2,1,0:T(8,128)(2,1)S(1)} %copy-done), custom_call_target="tpu_custom_call" | custom-call | flops 1073741824 | bytes 4194304 | tf_op jit(solution)/shard_map/to_rows/pallas_call | solution.py:274
  132.7 30.1 %all_to_all.35 = bf16[16,2,4,32,256]{4,3,2,1,0:T(8,128)(2,1)S(1)} all-to-all(bf16[16,2,4,32,256]{4,3,2,1,0:T(8,128)(2,1)S(1)} %to_rows.1), channel_id=1, replica_groups=mesh['kx'=8,'ky'=16] {'ky'}, dimensions={0} | all-to-all | bytes 4194304 | tf_op jit(solution)/shard_map/all_to_all | solution.py:283
  162.8 0.5 convert_bitcast_fusion
  163.3 2.3 %copy.5 = f32[2,16,4,32,256]{4,3,2,1,0:T(8,128)} copy(f32[2,16,4,32,256]{4,3,2,0,1:T(8,128)S(1)} %convert_bitcast_fusion) | data formatting | bytes 8388608 | tf_op jit(solution)/shard_map/convert_element_type | solution.py:284
Async XLA Ops:
  1.8 33.6 %copy-start = (bf16[4,2,512,512]{3,2,1,0:T(8,128)(2,1)S(1)}, bf16[4,2,512,512]{3,2,1,0:T(8,128)(2,1)}, u32[]{:S(2)}) copy-start(bf16[4,2,512,512]{3,2,1,0:T(8,128)(2,1)} %constant.2.clone.refs_1_) | copy-start | bytes 12582916
  38.1 38.8 %copy-start.1 = (bf16[2,12,256,256]{3,2,1,0:T(8,128)(2,1)S(1)}, bf16[2,12,256,256]{3,2,1,0:T(8,128)(2,1)}, u32[]{:S(2)}) copy-start(bf16[2,12,256,256]{3,2,1,0:T(8,128)(2,1)} %refs_2_.1) | copy-start | bytes 9437188

commit v5 on v4

--- a/solution.py
+++ b/solution.py
@@ -29,11 +29,12 @@
     return np.stack([np.stack([cos, -sin], 1), np.stack([sin, cos], 1)], 0)
 
 
-def tables(length, groups):
+def tables(length, groups, kx):
     quad = length // groups
     half = length // 2
     pairs = pair_list(length)
     low = np.arange(half)
+    sent = low.reshape(kx // 2, groups // kx, quad).transpose(1, 0, 2).reshape(-1)
     own = np.stack([pairs[:half].reshape(groups, -1), pairs[half:].reshape(groups, -1)], 1).reshape(groups, quad)
     found = []
     for parity in range(2):
@@ -42,8 +43,8 @@
         cols = quad // 2
         t_y = complex_table(y, low, length, 1.0, 1.0)
         t_y = t_y.reshape(2, cols, groups, 2, half).transpose(1, 0, 2, 3, 4)
-        t_x = complex_table(x, low, length, 1.0, 1.0 / length).transpose(0, 1, 3, 2)
-        b_x = complex_table(low, x, length, -1.0, 1.0).transpose(1, 0, 2, 3)
+        t_x = complex_table(x, sent, length, 1.0, 1.0 / length).transpose(0, 1, 3, 2)
+        b_x = complex_table(sent, x, length, -1.0, 1.0).transpose(1, 0, 2, 3)
         b_y = complex_table(low, y, length, -1.0, 1.0 / length)
         b_y = b_y.reshape(2, half, 2, cols, groups).transpose(0, 1, 3, 2, 4)
         found.append([t.reshape(length, length) for t in (t_y, t_x, b_x, b_y)])
@@ -100,13 +101,15 @@
     ref[col, 2 * c + 1, :TILE, :] = jnp.where(top, low, high)
 
 
-def sites_kernel(quad, freqs, bosons, block_ref, table_ref, vertex_ref, out_ref, green_ref, field_ref, mixed_ref):
+def sites_kernel(quad, kx, freqs, bosons, block_ref, table_ref, vertex_ref, out_ref, green_ref, field_ref, mixed_ref):
     half = green_ref.shape[2]
     length = 2 * half
     part = half // 2
     first = lax.axis_index("kx") + lax.axis_index("ky") == 0
 
-    low, high = block_ref[:length, :], block_ref[length:, :]
+    run = kx * quad
+    sent = block_ref[...].reshape(length // run, 2, run, quad * freqs)
+    low, high = [sent[:, i].reshape(length, quad * freqs) for i in range(2)]
     for parity in range(2):
         lattice = dot(table_ref[1, parity], low - high if parity else low + high).astype(jnp.bfloat16)
         for at in range(4):
@@ -182,8 +185,11 @@
             )
             for parity in range(2)
         ]
-        out_ref[:length, lanes] = (even + odd).astype(jnp.bfloat16)
-        out_ref[length:, lanes] = (even - odd).astype(jnp.bfloat16)
+        for upper, total in ((0, even + odd), (1, even - odd)):
+            total = total.astype(jnp.bfloat16)
+            for k in range(length // run):
+                at = (2 * k + upper) * run
+                out_ref[at : at + run, lanes] = total[k * run : (k + 1) * run]
 
 
 def rows_kernel(quad, groups, freqs, block_ref, table_ref, out_ref, wide_ref, rhs_ref):
@@ -220,6 +226,18 @@
     lax.fori_loop(0, quad, row, 0)
 
 
+def settle_kernel(devices, quad, block_ref, out_hbm, wide_ref, sems):
+    copies = []
+    for c in range(2):
+        for d in range(devices):
+            wide_ref[c, d] = block_ref[d, c].astype(jnp.float32)
+            copy = pltpu.make_async_copy(wide_ref.at[c, d], out_hbm.at[c, pl.ds(d * quad, quad)], sems.at[c, d])
+            copy.start()
+            copies.append(copy)
+    for copy in copies:
+        copy.wait()
+
+
 def in_vmem():
     return pl.BlockSpec(memory_space=pltpu.VMEM)
 
@@ -245,8 +263,8 @@
     quad = length // groups
     bosons = vertex.shape[1]
     n = 2 * length
-    dfts = jnp.asarray(tables(length, groups))
-    both = ("kx", "ky")
+    dfts = jnp.asarray(tables(length, groups, kx))
+    both = ("ky", "kx")
 
     block = green.reshape(2, ky, quad, width, freqs).transpose(1, 0, 2, 3, 4)
     block = lax.all_to_all(block, "ky", split_axis=0, concat_axis=0, tiled=True)
@@ -261,7 +279,7 @@
     )(block, dfts)
     spectrum = lax.all_to_all(spectrum, both, split_axis=0, concat_axis=0, tiled=True)
     field = call(
-        lambda *refs: sites_kernel(quad, freqs, bosons, *refs),
+        lambda *refs: sites_kernel(quad, kx, freqs, bosons, *refs),
         (n, quad * freqs),
         [in_vmem()] * 3,
         [pltpu.VMEM((quad, 4, length // 2, freqs), jnp.bfloat16)] * 2
@@ -281,7 +299,18 @@
         "to_rows",
     )(field, dfts)
     settled = lax.all_to_all(settled, "ky", split_axis=0, concat_axis=0, tiled=True)
-    return settled.transpose(1, 0, 2, 3, 4).reshape(2, rows, width, freqs).astype(jnp.float32)
+    return pl.pallas_call(
+        lambda *refs: settle_kernel(ky, quad, *refs),
+        out_shape=jax.ShapeDtypeStruct((2, rows, width, freqs), jnp.float32),
+        in_specs=[in_vmem()],
+        out_specs=pl.BlockSpec(memory_space=pltpu.HBM),
+        scratch_shapes=[
+            pltpu.VMEM((2, ky, quad, width, freqs), jnp.float32),
+            pltpu.SemaphoreType.DMA((2, ky)),
+        ],
+        compiler_params=pltpu.CompilerParams(vmem_limit_bytes=12 * 2**20),
+        name="to_output",
+    )(settled)
 
 
 def solution(mesh):

time: 166 us -> 164 us (0.988)
  local copies, waits for them, and re-layouts: 4.11 us -> 1.77 us
  Pallas kernels: 23.5 us -> 25.8 us
  blocking collectives: 138 us -> 136 us
    convert_element_type x1 -> x0, local copies, waits for them, and re-layouts: 2.34 us -> none  [per_device(): settled.transpose(1, 0, 2, 3, 4).reshape(2, rows, width, freqs)]
    pallas_call x1 -> x2, Pallas kernels: 17.7 us -> 20 us  [the longest x1 17.8 us: per_device(): call(lambda *refs: sites_kernel(quad, kx, freqs, bosons, *refs), (n, quad...]
where the time goes in v5:
time: 164 us
  blocking collectives  136 us (83%)
  Pallas kernels  25.8 us (16%)
  local copies, waits for them, and re-layouts  1.77 us (1%)
    all_to_all x1, blocking collectives, per_device(): lax.all_to_all(spectrum, both, split_axis=0, concat_axis=0, tiled=True)  37.2 us
    all_to_all x1, blocking collectives, per_device(): field = lax.all_to_all(field, both, split_axis=0, concat_axis=0, tiled=True)  34.3 us
    all_to_all x1, blocking collectives, per_device(): block = lax.all_to_all(block, 'ky', split_axis=0, concat_axis=0, tiled=True)  33.6 us
    all_to_all x1, blocking collectives, per_device(): lax.all_to_all(settled, 'ky', split_axis=0, concat_axis=0, tiled=True)  31.4 us
    pallas_call x1, Pallas kernels, per_device(): call(lambda *refs: sites_kernel(quad, kx, freqs, bosons, *refs), (n, quad...  17.8 us

profile of v5, /device:TPU:1, one launch (start us, length us, event | category | flops | bytes accessed | tf_op | source)
XLA Modules:
  0.0 164.1 jit_solution(6776594948791130459)
XLA Ops:
  0.0 1.8 %copy.6 = bf16[2,16,4,32,256]{4,3,2,0,1:T(8,128)(2,1)S(1)} copy(bf16[2,16,4,32,256]{4,3,2,1,0:T(8,128)(2,1)} %bitcast.13) | data formatting | bytes 4194304 | tf_op jit(solution)/shard_map/reshape | solution.py:269
  1.8 0.0 copy-start
  1.8 33.6 %all_to_all.32.refs_0_ = bf16[16,2,4,32,256]{4,3,2,1,0:T(8,128)(2,1)S(1)} all-to-all(bf16[16,2,4,32,256]{4,3,2,1,0:T(8,128)(2,1)S(1)} %bitcast.12), channel_id=1, replica_groups=mesh['kx'=8,'ky'=16] {'ky'}, dimensions={0} | all-to-all | bytes 4194304 | tf_op jit(solution)/shard_map/all_to_all | solution.py:270
  35.4 0.0 copy-done
  35.4 2.7 %to_columns.1 = bf16[1024,1024]{1,0:T(8,128)(2,1)S(1)} custom-call(bf16[16,2,4,32,256]{4,3,2,1,0:T(8,128)(2,1)S(1)} %all_to_all.32.refs_0_, bf16[4,2,512,512]{3,2,1,0:T(8,128)(2,1)S(1)} %copy-done), custom_call_target="tpu_custom_call" | custom-call | flops 1073741824 | bytes 4194304 | tf_op jit(solution)/shard_map/to_columns/pallas_call | solution.py:271
  38.1 0.0 copy-start.1
  38.1 37.2 %all_to_all.33 = bf16[128,8,1024]{2,1,0:T(8,128)(2,1)S(1)} all-to-all(bf16[128,8,1024]{2,1,0:T(8,128)(2,1)S(1)} %bitcast.9), channel_id=1, replica_groups=mesh['kx'=8,'ky'=16] {'ky','kx'}, dimensions={0} | all-to-all | bytes 4194304 | tf_op jit(solution)/shard_map/all_to_all | solution.py:280
  75.3 0.0 copy-done.1
  75.3 17.8 %on_sites.1 = bf16[1024,1024]{1,0:T(8,128)(2,1)S(1)} custom-call(bf16[1024,1024]{1,0:T(8,128)(2,1)S(1)} %bitcast.10, bf16[4,2,512,512]{3,2,1,0:T(8,128)(2,1)S(1)} %copy-done, bf16[2,12,256,256]{3,2,1,0:T(8,128)(2,1)S(1)} %copy-done.1), custom_call_target="tpu_custom_call" | custom-call | flops 11811160064 | bytes 4194304 | tf_op jit(solution)/shard_map/on_sites/pallas_call | solution.py:281
  93.1 34.3 %all_to_all.34 = bf16[128,8,1024]{2,1,0:T(8,128)(2,1)S(1)} all-to-all(bf16[128,8,1024]{2,1,0:T(8,128)(2,1)S(1)} %bitcast.11), channel_id=1, replica_groups=mesh['kx'=8,'ky'=16] {'ky','kx'}, dimensions={0} | all-to-all | bytes 4194304 | tf_op jit(solution)/shard_map/all_to_all | solution.py:291
  127.4 3.0 %to_rows.1 = bf16[16,2,4,32,256]{4,3,2,1,0:T(8,128)(2,1)S(1)} custom-call(bf16[1024,1024]{1,0:T(8,128)(2,1)S(1)} %bitcast.8, bf16[4,2,512,512]{3,2,1,0:T(8,128)(2,1)S(1)} %copy-done), custom_call_target="tpu_custom_call" | custom-call | flops 1073741824 | bytes 4194304 | tf_op jit(solution)/shard_map/to_rows/pallas_call | solution.py:292
  130.4 31.4 %all_to_all.35.refs_0_ = bf16[16,2,4,32,256]{4,3,2,1,0:T(8,128)(2,1)S(1)} all-to-all(bf16[16,2,4,32,256]{4,3,2,1,0:T(8,128)(2,1)S(1)} %to_rows.1), channel_id=1, replica_groups=mesh['kx'=8,'ky'=16] {'ky'}, dimensions={0} | all-to-all | bytes 4194304 | tf_op jit(solution)/shard_map/all_to_all | solution.py:301
  161.8 2.3 %to_output.1 = f32[2,64,32,256]{3,2,1,0:T(8,128)} custom-call(bf16[16,2,4,32,256]{4,3,2,1,0:T(8,128)(2,1)S(1)} %all_to_all.35.refs_0_), custom_call_target="tpu_custom_call" | custom-call | tf_op jit(solution)/shard_map/to_output/pallas_call | solution.py:302
Async XLA Ops:
  1.8 33.6 %copy-start = (bf16[4,2,512,512]{3,2,1,0:T(8,128)(2,1)S(1)}, bf16[4,2,512,512]{3,2,1,0:T(8,128)(2,1)}, u32[]{:S(2)}) copy-start(bf16[4,2,512,512]{3,2,1,0:T(8,128)(2,1)} %constant.2.clone.refs_1_) | copy-start | bytes 12582916
  38.1 37.2 %copy-start.1 = (bf16[2,12,256,256]{3,2,1,0:T(8,128)(2,1)S(1)}, bf16[2,12,256,256]{3,2,1,0:T(8,128)(2,1)}, u32[]{:S(2)}) copy-start(bf16[2,12,256,256]{3,2,1,0:T(8,128)(2,1)} %refs_2_.1) | copy-start | bytes 9437188

commit v6 on v5

--- a/solution.py
+++ b/solution.py
@@ -76,7 +76,8 @@
                     wide_ref[col * (freqs // LANES) + k, spots, :] = part[:, k * LANES : (k + 1) * LANES]
         return carry
 
-    lax.fori_loop(0, quad, row, 0)
+    for r in range(quad):
+        row(r, 0)
 
     def settle(i, carry):
         at = pl.ds(pl.multiple_of(i * 128, 128), 128)
@@ -210,9 +211,9 @@
                 m = (col % 2) * length + ((col // 2) * 2 + c) * groups
                 for k in range(freqs // LANES):
                     part = wide_ref[col * (freqs // LANES) + k, pl.ds(r * 2 + c, groups, stride=2 * quad), :]
-                    rhs_ref[m : m + groups, k * LANES : (k + 1) * LANES] = part.astype(jnp.bfloat16)
+                    rhs_ref[r, m : m + groups, k * LANES : (k + 1) * LANES] = part.astype(jnp.bfloat16)
         even, odd = [
-            dot(table_ref[3, parity], rhs_ref[parity * length : (parity + 1) * length, :]) for parity in range(2)
+            dot(table_ref[3, parity], rhs_ref[r, parity * length : (parity + 1) * length, :]) for parity in range(2)
         ]
         for upper, total in ((0, even + odd), (1, even - odd)):
             total = total.astype(jnp.bfloat16)
@@ -223,7 +224,8 @@
                 )
         return carry
 
-    lax.fori_loop(0, quad, row, 0)
+    for r in range(quad):
+        row(r, 0)
 
 
 def settle_kernel(devices, quad, block_ref, out_hbm, wide_ref, sems):
@@ -293,7 +295,7 @@
         lambda *refs: rows_kernel(quad, groups, freqs, *refs),
         (ky, 2, quad, width, freqs),
         [in_vmem()] * 2,
-        [pltpu.VMEM((quad * freqs // LANES, n, LANES), jnp.float32), pltpu.VMEM((n, freqs), jnp.bfloat16)],
+        [pltpu.VMEM((quad * freqs // LANES, n, LANES), jnp.float32), pltpu.VMEM((quad, n, freqs), jnp.bfloat16)],
         n * n * quad * freqs,
         16,
         "to_rows",

time: 164 us -> 163 us (level)
  no operation moved by 1% of the time
where the time goes in v6:
time: 163 us
  blocking collectives  137 us (84%)
  Pallas kernels  24.6 us (15%)
  local copies, waits for them, and re-layouts  1.77 us (1%)
    all_to_all x1, blocking collectives, per_device(): lax.all_to_all(spectrum, both, split_axis=0, concat_axis=0, tiled=True)  37.2 us
    all_to_all x1, blocking collectives, per_device(): field = lax.all_to_all(field, both, split_axis=0, concat_axis=0, tiled=True)  34.3 us
    all_to_all x1, blocking collectives, per_device(): block = lax.all_to_all(block, 'ky', split_axis=0, concat_axis=0, tiled=True)  33.6 us
    all_to_all x1, blocking collectives, per_device(): lax.all_to_all(settled, 'ky', split_axis=0, concat_axis=0, tiled=True)  31.4 us
    pallas_call x1, Pallas kernels, per_device(): call(lambda *refs: sites_kernel(quad, kx, freqs, bosons, *refs), (n, quad...  17.8 us

profile of v6, /device:TPU:1, one launch (start us, length us, event | category | flops | bytes accessed | tf_op | source)
XLA Modules:
  0.0 162.9 jit_solution(714098070739391586)
XLA Ops:
  0.0 1.8 %copy.6 = bf16[2,16,4,32,256]{4,3,2,0,1:T(8,128)(2,1)S(1)} copy(bf16[2,16,4,32,256]{4,3,2,1,0:T(8,128)(2,1)} %bitcast.13) | data formatting | bytes 4194304 | tf_op jit(solution)/shard_map/reshape | solution.py:271
  1.8 0.0 copy-start
  1.8 33.6 %all_to_all.32.refs_0_ = bf16[16,2,4,32,256]{4,3,2,1,0:T(8,128)(2,1)S(1)} all-to-all(bf16[16,2,4,32,256]{4,3,2,1,0:T(8,128)(2,1)S(1)} %bitcast.12), channel_id=1, replica_groups=mesh['kx'=8,'ky'=16] {'ky'}, dimensions={0} | all-to-all | bytes 4194304 | tf_op jit(solution)/shard_map/all_to_all | solution.py:272
  35.4 0.0 copy-done
  35.4 2.3 %to_columns.1 = bf16[1024,1024]{1,0:T(8,128)(2,1)S(1)} custom-call(bf16[16,2,4,32,256]{4,3,2,1,0:T(8,128)(2,1)S(1)} %all_to_all.32.refs_0_, bf16[4,2,512,512]{3,2,1,0:T(8,128)(2,1)S(1)} %copy-done), custom_call_target="tpu_custom_call" | custom-call | flops 1073741824 | bytes 4194304 | tf_op jit(solution)/shard_map/to_columns/pallas_call | solution.py:273
  37.7 0.0 copy-start.1
  37.7 37.2 %all_to_all.33 = bf16[128,8,1024]{2,1,0:T(8,128)(2,1)S(1)} all-to-all(bf16[128,8,1024]{2,1,0:T(8,128)(2,1)S(1)} %bitcast.9), channel_id=1, replica_groups=mesh['kx'=8,'ky'=16] {'ky','kx'}, dimensions={0} | all-to-all | bytes 4194304 | tf_op jit(solution)/shard_map/all_to_all | solution.py:282
  74.9 0.0 copy-done.1
  74.9 17.8 %on_sites.1 = bf16[1024,1024]{1,0:T(8,128)(2,1)S(1)} custom-call(bf16[1024,1024]{1,0:T(8,128)(2,1)S(1)} %bitcast.10, bf16[4,2,512,512]{3,2,1,0:T(8,128)(2,1)S(1)} %copy-done, bf16[2,12,256,256]{3,2,1,0:T(8,128)(2,1)S(1)} %copy-done.1), custom_call_target="tpu_custom_call" | custom-call | flops 11811160064 | bytes 4194304 | tf_op jit(solution)/shard_map/on_sites/pallas_call | solution.py:283
  92.7 34.3 %all_to_all.34 = bf16[128,8,1024]{2,1,0:T(8,128)(2,1)S(1)} all-to-all(bf16[128,8,1024]{2,1,0:T(8,128)(2,1)S(1)} %bitcast.11), channel_id=1, replica_groups=mesh['kx'=8,'ky'=16] {'ky','kx'}, dimensions={0} | all-to-all | bytes 4194304 | tf_op jit(solution)/shard_map/all_to_all | solution.py:293
  127.0 2.3 %to_rows.1 = bf16[16,2,4,32,256]{4,3,2,1,0:T(8,128)(2,1)S(1)} custom-call(bf16[1024,1024]{1,0:T(8,128)(2,1)S(1)} %bitcast.8, bf16[4,2,512,512]{3,2,1,0:T(8,128)(2,1)S(1)} %copy-done), custom_call_target="tpu_custom_call" | custom-call | flops 1073741824 | bytes 4194304 | tf_op jit(solution)/shard_map/to_rows/pallas_call | solution.py:294
  129.2 31.4 %all_to_all.35.refs_0_ = bf16[16,2,4,32,256]{4,3,2,1,0:T(8,128)(2,1)S(1)} all-to-all(bf16[16,2,4,32,256]{4,3,2,1,0:T(8,128)(2,1)S(1)} %to_rows.1), channel_id=1, replica_groups=mesh['kx'=8,'ky'=16] {'ky'}, dimensions={0} | all-to-all | bytes 4194304 | tf_op jit(solution)/shard_map/all_to_all | solution.py:303
  160.6 2.3 %to_output.1 = f32[2,64,32,256]{3,2,1,0:T(8,128)} custom-call(bf16[16,2,4,32,256]{4,3,2,1,0:T(8,128)(2,1)S(1)} %all_to_all.35.refs_0_), custom_call_target="tpu_custom_call" | custom-call | tf_op jit(solution)/shard_map/to_output/pallas_call | solution.py:304
Async XLA Ops:
  1.8 33.6 %copy-start = (bf16[4,2,512,512]{3,2,1,0:T(8,128)(2,1)S(1)}, bf16[4,2,512,512]{3,2,1,0:T(8,128)(2,1)}, u32[]{:S(2)}) copy-start(bf16[4,2,512,512]{3,2,1,0:T(8,128)(2,1)} %constant.2.clone.refs_1_) | copy-start | bytes 12582916
  37.7 37.2 %copy-start.1 = (bf16[2,12,256,256]{3,2,1,0:T(8,128)(2,1)S(1)}, bf16[2,12,256,256]{3,2,1,0:T(8,128)(2,1)}, u32[]{:S(2)}) copy-start(bf16[2,12,256,256]{3,2,1,0:T(8,128)(2,1)} %refs_2_.1) | copy-start | bytes 9437188

commit v7 on v6

--- a/solution.py
+++ b/solution.py
@@ -11,7 +11,7 @@
 
 LANES = 128
 TILE = 16
-GROUP = 4
+GROUP = 6
 
 
 def pair_list(length):
@@ -85,7 +85,7 @@
             out_ref[at, k * LANES : (k + 1) * LANES] = wide_ref[k, at, :].astype(jnp.bfloat16)
         return carry
 
-    lax.fori_loop(0, 2 * length // 128, settle, 0)
+    lax.fori_loop(0, 2 * length // 128, settle, 0, unroll=True)
 
 
 def shifted(values, by):
@@ -153,9 +153,14 @@
                     b_re.append(g_re * m_re - g_im * m_im)
                     b_im.append(g_re * m_im + g_im * m_re)
                 b_re, b_im = jnp.concatenate(b_re, 0), jnp.concatenate(b_im, 0)
-                shared = dot_turned(b_re + b_im, vertex_ref[0, w])
-                c_re = (shared - dot_turned(b_im, mixed_ref[1, w])).astype(jnp.bfloat16)
-                c_im = (shared + dot_turned(b_re, mixed_ref[0, w])).astype(jnp.bfloat16)
+                if w % 2:
+                    panel = jnp.concatenate([vertex_ref[0, w], vertex_ref[1, w]], 1)
+                    c_re = dot_turned(jnp.concatenate([b_re, -b_im], 1), panel).astype(jnp.bfloat16)
+                    c_im = dot_turned(jnp.concatenate([b_im, b_re], 1), panel).astype(jnp.bfloat16)
+                else:
+                    shared = dot_turned(b_re + b_im, vertex_ref[0, w])
+                    c_re = (shared - dot_turned(b_im, mixed_ref[1, w])).astype(jnp.bfloat16)
+                    c_im = (shared + dot_turned(b_re, mixed_ref[0, w])).astype(jnp.bfloat16)
                 cp_re, cq_re, cp_im, cq_im = c_re[:half], c_re[half:], c_im[:half], c_im[half:]
                 terms = [
                     sp_re * cp_re - sp_im * cp_im,
@@ -203,7 +208,7 @@
             wide_ref[k, at, :] = block_ref[at, k * LANES : (k + 1) * LANES].astype(jnp.float32)
         return carry
 
-    lax.fori_loop(0, 2 * length // 128, widen, 0)
+    lax.fori_loop(0, 2 * length // 128, widen, 0, unroll=True)
 
     def row(r, carry):
         for col in range(quad):

time: 163 us -> 162 us (level)
  no operation moved by 1% of the time
where the time goes in v7:
time: 162 us
  blocking collectives  136 us (84%)
  Pallas kernels  24 us (15%)
  local copies, waits for them, and re-layouts  1.77 us (1%)
    all_to_all x1, blocking collectives, per_device(): lax.all_to_all(spectrum, both, split_axis=0, concat_axis=0, tiled=True)  37.2 us
    all_to_all x1, blocking collectives, per_device(): field = lax.all_to_all(field, both, split_axis=0, concat_axis=0, tiled=True)  34.3 us
    all_to_all x1, blocking collectives, per_device(): block = lax.all_to_all(block, 'ky', split_axis=0, concat_axis=0, tiled=True)  33.6 us
    all_to_all x1, blocking collectives, per_device(): lax.all_to_all(settled, 'ky', split_axis=0, concat_axis=0, tiled=True)  31.4 us
    pallas_call x1, Pallas kernels, per_device(): call(lambda *refs: sites_kernel(quad, kx, freqs, bosons, *refs), (n, quad...  17.3 us

profile of v7, /device:TPU:1, one launch (start us, length us, event | category | flops | bytes accessed | tf_op | source)
XLA Modules:
  0.0 162.3 jit_solution(16568590682118067995)
XLA Ops:
  0.0 1.8 %copy.6 = bf16[2,16,4,32,256]{4,3,2,0,1:T(8,128)(2,1)S(1)} copy(bf16[2,16,4,32,256]{4,3,2,1,0:T(8,128)(2,1)} %bitcast.13) | data formatting | bytes 4194304 | tf_op jit(solution)/shard_map/reshape | solution.py:276
  1.8 0.0 copy-start
  1.8 33.6 %all_to_all.32.refs_0_ = bf16[16,2,4,32,256]{4,3,2,1,0:T(8,128)(2,1)S(1)} all-to-all(bf16[16,2,4,32,256]{4,3,2,1,0:T(8,128)(2,1)S(1)} %bitcast.12), channel_id=1, replica_groups=mesh['kx'=8,'ky'=16] {'ky'}, dimensions={0} | all-to-all | bytes 4194304 | tf_op jit(solution)/shard_map/all_to_all | solution.py:277
  35.4 0.0 copy-done
  35.4 2.2 %to_columns.1 = bf16[1024,1024]{1,0:T(8,128)(2,1)S(1)} custom-call(bf16[16,2,4,32,256]{4,3,2,1,0:T(8,128)(2,1)S(1)} %all_to_all.32.refs_0_, bf16[4,2,512,512]{3,2,1,0:T(8,128)(2,1)S(1)} %copy-done), custom_call_target="tpu_custom_call" | custom-call | flops 1073741824 | bytes 4194304 | tf_op jit(solution)/shard_map/to_columns/pallas_call | solution.py:278
  37.6 0.0 copy-start.1
  37.6 37.2 %all_to_all.33 = bf16[128,8,1024]{2,1,0:T(8,128)(2,1)S(1)} all-to-all(bf16[128,8,1024]{2,1,0:T(8,128)(2,1)S(1)} %bitcast.9), channel_id=1, replica_groups=mesh['kx'=8,'ky'=16] {'ky','kx'}, dimensions={0} | all-to-all | bytes 4194304 | tf_op jit(solution)/shard_map/all_to_all | solution.py:287
  74.8 0.0 copy-done.1
  74.8 17.3 %on_sites.1 = bf16[1024,1024]{1,0:T(8,128)(2,1)S(1)} custom-call(bf16[1024,1024]{1,0:T(8,128)(2,1)S(1)} %bitcast.10, bf16[4,2,512,512]{3,2,1,0:T(8,128)(2,1)S(1)} %copy-done, bf16[2,12,256,256]{3,2,1,0:T(8,128)(2,1)S(1)} %copy-done.1), custom_call_target="tpu_custom_call" | custom-call | flops 11811160064 | bytes 4194304 | tf_op jit(solution)/shard_map/on_sites/pallas_call | solution.py:288
  92.1 34.3 %all_to_all.34 = bf16[128,8,1024]{2,1,0:T(8,128)(2,1)S(1)} all-to-all(bf16[128,8,1024]{2,1,0:T(8,128)(2,1)S(1)} %bitcast.11), channel_id=1, replica_groups=mesh['kx'=8,'ky'=16] {'ky','kx'}, dimensions={0} | all-to-all | bytes 4194304 | tf_op jit(solution)/shard_map/all_to_all | solution.py:298
  126.4 2.2 %to_rows.1 = bf16[16,2,4,32,256]{4,3,2,1,0:T(8,128)(2,1)S(1)} custom-call(bf16[1024,1024]{1,0:T(8,128)(2,1)S(1)} %bitcast.8, bf16[4,2,512,512]{3,2,1,0:T(8,128)(2,1)S(1)} %copy-done), custom_call_target="tpu_custom_call" | custom-call | flops 1073741824 | bytes 4194304 | tf_op jit(solution)/shard_map/to_rows/pallas_call | solution.py:299
  128.6 31.4 %all_to_all.35.refs_0_ = bf16[16,2,4,32,256]{4,3,2,1,0:T(8,128)(2,1)S(1)} all-to-all(bf16[16,2,4,32,256]{4,3,2,1,0:T(8,128)(2,1)S(1)} %to_rows.1), channel_id=1, replica_groups=mesh['kx'=8,'ky'=16] {'ky'}, dimensions={0} | all-to-all | bytes 4194304 | tf_op jit(solution)/shard_map/all_to_all | solution.py:308
  160.0 2.3 %to_output.1 = f32[2,64,32,256]{3,2,1,0:T(8,128)} custom-call(bf16[16,2,4,32,256]{4,3,2,1,0:T(8,128)(2,1)S(1)} %all_to_all.35.refs_0_), custom_call_target="tpu_custom_call" | custom-call | tf_op jit(solution)/shard_map/to_output/pallas_call | solution.py:309
Async XLA Ops:
  1.8 33.6 %copy-start = (bf16[4,2,512,512]{3,2,1,0:T(8,128)(2,1)S(1)}, bf16[4,2,512,512]{3,2,1,0:T(8,128)(2,1)}, u32[]{:S(2)}) copy-start(bf16[4,2,512,512]{3,2,1,0:T(8,128)(2,1)} %constant.2.clone.refs_1_) | copy-start | bytes 12582916
  37.6 37.2 %copy-start.1 = (bf16[2,12,256,256]{3,2,1,0:T(8,128)(2,1)S(1)}, bf16[2,12,256,256]{3,2,1,0:T(8,128)(2,1)}, u32[]{:S(2)}) copy-start(bf16[2,12,256,256]{3,2,1,0:T(8,128)(2,1)} %refs_2_.1) | copy-start | bytes 9437188

commit v8 on v7

--- a/solution.py
+++ b/solution.py
@@ -11,6 +11,7 @@
 
 LANES = 128
 TILE = 16
+PIECES = 4
 GROUP = 6
 
 
@@ -233,12 +234,15 @@
         row(r, 0)
 
 
-def settle_kernel(devices, quad, block_ref, out_hbm, wide_ref, sems):
+def settle_kernel(devices, block_ref, out_hbm, wide_ref, sems):
+    few = devices // PIECES
     copies = []
     for c in range(2):
-        for d in range(devices):
-            wide_ref[c, d] = block_ref[d, c].astype(jnp.float32)
-            copy = pltpu.make_async_copy(wide_ref.at[c, d], out_hbm.at[c, pl.ds(d * quad, quad)], sems.at[c, d])
+        for i in range(PIECES):
+            for d in range(i * few, (i + 1) * few):
+                wide_ref[c, d] = block_ref[d, c].astype(jnp.float32)
+            at = pl.ds(i * few, few)
+            copy = pltpu.make_async_copy(wide_ref.at[c, at], out_hbm.at[c, at], sems.at[c, i])
             copy.start()
             copies.append(copy)
     for copy in copies:
@@ -307,17 +311,17 @@
     )(field, dfts)
     settled = lax.all_to_all(settled, "ky", split_axis=0, concat_axis=0, tiled=True)
     return pl.pallas_call(
-        lambda *refs: settle_kernel(ky, quad, *refs),
-        out_shape=jax.ShapeDtypeStruct((2, rows, width, freqs), jnp.float32),
+        lambda *refs: settle_kernel(ky, *refs),
+        out_shape=jax.ShapeDtypeStruct((2, ky, quad, width, freqs), jnp.float32),
         in_specs=[in_vmem()],
         out_specs=pl.BlockSpec(memory_space=pltpu.HBM),
         scratch_shapes=[
             pltpu.VMEM((2, ky, quad, width, freqs), jnp.float32),
-            pltpu.SemaphoreType.DMA((2, ky)),
+            pltpu.SemaphoreType.DMA((2, PIECES)),
         ],
         compiler_params=pltpu.CompilerParams(vmem_limit_bytes=12 * 2**20),
         name="to_output",
-    )(settled)
+    )(settled).reshape(2, rows, width, freqs)
 
 
 def solution(mesh):

time: 162 us -> 162 us (level)
  no operation moved by 1% of the time
where the time goes in v8:
time: 162 us
  blocking collectives  136 us (84%)
  Pallas kernels  23.8 us (15%)
  local copies, waits for them, and re-layouts  1.77 us (1%)
    all_to_all x1, blocking collectives, per_device(): lax.all_to_all(spectrum, both, split_axis=0, concat_axis=0, tiled=True)  37.2 us
    all_to_all x1, blocking collectives, per_device(): field = lax.all_to_all(field, both, split_axis=0, concat_axis=0, tiled=True)  34.3 us
    all_to_all x1, blocking collectives, per_device(): block = lax.all_to_all(block, 'ky', split_axis=0, concat_axis=0, tiled=True)  33.6 us
    all_to_all x1, blocking collectives, per_device(): lax.all_to_all(settled, 'ky', split_axis=0, concat_axis=0, tiled=True)  31.4 us
    pallas_call x1, Pallas kernels, per_device(): call(lambda *refs: sites_kernel(quad, kx, freqs, bosons, *refs), (n, quad...  17.3 us

profile of v8, /device:TPU:1, one launch (start us, length us, event | category | flops | bytes accessed | tf_op | source)
XLA Modules:
  0.0 162.1 jit_solution(8078611944719768624)
XLA Ops:
  0.0 1.8 %copy.6 = bf16[2,16,4,32,256]{4,3,2,0,1:T(8,128)(2,1)S(1)} copy(bf16[2,16,4,32,256]{4,3,2,1,0:T(8,128)(2,1)} %bitcast.14) | data formatting | bytes 4194304 | tf_op jit(solution)/shard_map/reshape | solution.py:280
  1.8 0.0 copy-start
  1.8 33.6 %all_to_all.32.refs_0_ = bf16[16,2,4,32,256]{4,3,2,1,0:T(8,128)(2,1)S(1)} all-to-all(bf16[16,2,4,32,256]{4,3,2,1,0:T(8,128)(2,1)S(1)} %bitcast.13), channel_id=1, replica_groups=mesh['kx'=8,'ky'=16] {'ky'}, dimensions={0} | all-to-all | bytes 4194304 | tf_op jit(solution)/shard_map/all_to_all | solution.py:281
  35.4 0.0 copy-done
  35.4 2.2 %to_columns.1 = bf16[1024,1024]{1,0:T(8,128)(2,1)S(1)} custom-call(bf16[16,2,4,32,256]{4,3,2,1,0:T(8,128)(2,1)S(1)} %all_to_all.32.refs_0_, bf16[4,2,512,512]{3,2,1,0:T(8,128)(2,1)S(1)} %copy-done), custom_call_target="tpu_custom_call" | custom-call | flops 1073741824 | bytes 4194304 | tf_op jit(solution)/shard_map/to_columns/pallas_call | solution.py:282
  37.6 0.0 copy-start.1
  37.6 37.2 %all_to_all.33 = bf16[128,8,1024]{2,1,0:T(8,128)(2,1)S(1)} all-to-all(bf16[128,8,1024]{2,1,0:T(8,128)(2,1)S(1)} %bitcast.10), channel_id=1, replica_groups=mesh['kx'=8,'ky'=16] {'ky','kx'}, dimensions={0} | all-to-all | bytes 4194304 | tf_op jit(solution)/shard_map/all_to_all | solution.py:291
  74.8 0.0 copy-done.1
  74.8 17.3 %on_sites.1 = bf16[1024,1024]{1,0:T(8,128)(2,1)S(1)} custom-call(bf16[1024,1024]{1,0:T(8,128)(2,1)S(1)} %bitcast.11, bf16[4,2,512,512]{3,2,1,0:T(8,128)(2,1)S(1)} %copy-done, bf16[2,12,256,256]{3,2,1,0:T(8,128)(2,1)S(1)} %copy-done.1), custom_call_target="tpu_custom_call" | custom-call | flops 11811160064 | bytes 4194304 | tf_op jit(solution)/shard_map/on_sites/pallas_call | solution.py:292
  92.1 34.3 %all_to_all.34 = bf16[128,8,1024]{2,1,0:T(8,128)(2,1)S(1)} all-to-all(bf16[128,8,1024]{2,1,0:T(8,128)(2,1)S(1)} %bitcast.12), channel_id=1, replica_groups=mesh['kx'=8,'ky'=16] {'ky','kx'}, dimensions={0} | all-to-all | bytes 4194304 | tf_op jit(solution)/shard_map/all_to_all | solution.py:302
  126.4 2.2 %to_rows.1 = bf16[16,2,4,32,256]{4,3,2,1,0:T(8,128)(2,1)S(1)} custom-call(bf16[1024,1024]{1,0:T(8,128)(2,1)S(1)} %bitcast.9, bf16[4,2,512,512]{3,2,1,0:T(8,128)(2,1)S(1)} %copy-done), custom_call_target="tpu_custom_call" | custom-call | flops 1073741824 | bytes 4194304 | tf_op jit(solution)/shard_map/to_rows/pallas_call | solution.py:303
  128.6 31.4 %all_to_all.35.refs_0_ = bf16[16,2,4,32,256]{4,3,2,1,0:T(8,128)(2,1)S(1)} all-to-all(bf16[16,2,4,32,256]{4,3,2,1,0:T(8,128)(2,1)S(1)} %to_rows.1), channel_id=1, replica_groups=mesh['kx'=8,'ky'=16] {'ky'}, dimensions={0} | all-to-all | bytes 4194304 | tf_op jit(solution)/shard_map/all_to_all | solution.py:312
  160.0 2.1 %to_output.1 = f32[2,16,4,32,256]{4,3,2,1,0:T(8,128)} custom-call(bf16[16,2,4,32,256]{4,3,2,1,0:T(8,128)(2,1)S(1)} %all_to_all.35.refs_0_), custom_call_target="tpu_custom_call" | custom-call | tf_op jit(solution)/shard_map/to_output/pallas_call | solution.py:313
Async XLA Ops:
  1.8 33.6 %copy-start = (bf16[4,2,512,512]{3,2,1,0:T(8,128)(2,1)S(1)}, bf16[4,2,512,512]{3,2,1,0:T(8,128)(2,1)}, u32[]{:S(2)}) copy-start(bf16[4,2,512,512]{3,2,1,0:T(8,128)(2,1)} %constant.2.clone.refs_1_) | copy-start | bytes 12582916
  37.6 37.2 %copy-start.1 = (bf16[2,12,256,256]{3,2,1,0:T(8,128)(2,1)S(1)}, bf16[2,12,256,256]{3,2,1,0:T(8,128)(2,1)}, u32[]{:S(2)}) copy-start(bf16[2,12,256,256]{3,2,1,0:T(8,128)(2,1)} %refs_2_.1) | copy-start | bytes 9437188

commit v9 on v8

--- a/solution.py
+++ b/solution.py
@@ -11,7 +11,7 @@
 
 LANES = 128
 TILE = 16
-PIECES = 4
+PIECES = 2
 GROUP = 6
 
 

time: 162 us -> 162 us (level)
  no operation moved by 1% of the time
where the time goes in v9:
time: 162 us
  blocking collectives  136 us (84%)
  Pallas kernels  23.8 us (15%)
  local copies, waits for them, and re-layouts  1.77 us (1%)
    all_to_all x1, blocking collectives, per_device(): lax.all_to_all(spectrum, both, split_axis=0, concat_axis=0, tiled=True)  37.2 us
    all_to_all x1, blocking collectives, per_device(): field = lax.all_to_all(field, both, split_axis=0, concat_axis=0, tiled=True)  34.3 us
    all_to_all x1, blocking collectives, per_device(): block = lax.all_to_all(block, 'ky', split_axis=0, concat_axis=0, tiled=True)  33.6 us
    all_to_all x1, blocking collectives, per_device(): lax.all_to_all(settled, 'ky', split_axis=0, concat_axis=0, tiled=True)  31.4 us
    pallas_call x1, Pallas kernels, per_device(): call(lambda *refs: sites_kernel(quad, kx, freqs, bosons, *refs), (n, quad...  17.3 us

profile of v9, /device:TPU:1, one launch (start us, length us, event | category | flops | bytes accessed | tf_op | source)
XLA Modules:
  0.0 162.1 jit_solution(13741779631689458939)
XLA Ops:
  0.0 1.8 %copy.6 = bf16[2,16,4,32,256]{4,3,2,0,1:T(8,128)(2,1)S(1)} copy(bf16[2,16,4,32,256]{4,3,2,1,0:T(8,128)(2,1)} %bitcast.14) | data formatting | bytes 4194304 | tf_op jit(solution)/shard_map/reshape | solution.py:280
  1.8 0.0 copy-start
  1.8 33.6 %all_to_all.32.refs_0_ = bf16[16,2,4,32,256]{4,3,2,1,0:T(8,128)(2,1)S(1)} all-to-all(bf16[16,2,4,32,256]{4,3,2,1,0:T(8,128)(2,1)S(1)} %bitcast.13), channel_id=1, replica_groups=mesh['kx'=8,'ky'=16] {'ky'}, dimensions={0} | all-to-all | bytes 4194304 | tf_op jit(solution)/shard_map/all_to_all | solution.py:281
  35.4 0.0 copy-done
  35.4 2.2 %to_columns.1 = bf16[1024,1024]{1,0:T(8,128)(2,1)S(1)} custom-call(bf16[16,2,4,32,256]{4,3,2,1,0:T(8,128)(2,1)S(1)} %all_to_all.32.refs_0_, bf16[4,2,512,512]{3,2,1,0:T(8,128)(2,1)S(1)} %copy-done), custom_call_target="tpu_custom_call" | custom-call | flops 1073741824 | bytes 4194304 | tf_op jit(solution)/shard_map/to_columns/pallas_call | solution.py:282
  37.6 0.0 copy-start.1
  37.6 37.2 %all_to_all.33 = bf16[128,8,1024]{2,1,0:T(8,128)(2,1)S(1)} all-to-all(bf16[128,8,1024]{2,1,0:T(8,128)(2,1)S(1)} %bitcast.10), channel_id=1, replica_groups=mesh['kx'=8,'ky'=16] {'ky','kx'}, dimensions={0} | all-to-all | bytes 4194304 | tf_op jit(solution)/shard_map/all_to_all | solution.py:291
  74.8 0.0 copy-done.1
  74.8 17.3 %on_sites.1 = bf16[1024,1024]{1,0:T(8,128)(2,1)S(1)} custom-call(bf16[1024,1024]{1,0:T(8,128)(2,1)S(1)} %bitcast.11, bf16[4,2,512,512]{3,2,1,0:T(8,128)(2,1)S(1)} %copy-done, bf16[2,12,256,256]{3,2,1,0:T(8,128)(2,1)S(1)} %copy-done.1), custom_call_target="tpu_custom_call" | custom-call | flops 11811160064 | bytes 4194304 | tf_op jit(solution)/shard_map/on_sites/pallas_call | solution.py:292
  92.1 34.3 %all_to_all.34 = bf16[128,8,1024]{2,1,0:T(8,128)(2,1)S(1)} all-to-all(bf16[128,8,1024]{2,1,0:T(8,128)(2,1)S(1)} %bitcast.12), channel_id=1, replica_groups=mesh['kx'=8,'ky'=16] {'ky','kx'}, dimensions={0} | all-to-all | bytes 4194304 | tf_op jit(solution)/shard_map/all_to_all | solution.py:302
  126.4 2.2 %to_rows.1 = bf16[16,2,4,32,256]{4,3,2,1,0:T(8,128)(2,1)S(1)} custom-call(bf16[1024,1024]{1,0:T(8,128)(2,1)S(1)} %bitcast.9, bf16[4,2,512,512]{3,2,1,0:T(8,128)(2,1)S(1)} %copy-done), custom_call_target="tpu_custom_call" | custom-call | flops 1073741824 | bytes 4194304 | tf_op jit(solution)/shard_map/to_rows/pallas_call | solution.py:303
  128.6 31.4 %all_to_all.35.refs_0_ = bf16[16,2,4,32,256]{4,3,2,1,0:T(8,128)(2,1)S(1)} all-to-all(bf16[16,2,4,32,256]{4,3,2,1,0:T(8,128)(2,1)S(1)} %to_rows.1), channel_id=1, replica_groups=mesh['kx'=8,'ky'=16] {'ky'}, dimensions={0} | all-to-all | bytes 4194304 | tf_op jit(solution)/shard_map/all_to_all | solution.py:312
  160.0 2.1 %to_output.1 = f32[2,16,4,32,256]{4,3,2,1,0:T(8,128)} custom-call(bf16[16,2,4,32,256]{4,3,2,1,0:T(8,128)(2,1)S(1)} %all_to_all.35.refs_0_), custom_call_target="tpu_custom_call" | custom-call | tf_op jit(solution)/shard_map/to_output/pallas_call | solution.py:313
Async XLA Ops:
  1.8 33.6 %copy-start = (bf16[4,2,512,512]{3,2,1,0:T(8,128)(2,1)S(1)}, bf16[4,2,512,512]{3,2,1,0:T(8,128)(2,1)}, u32[]{:S(2)}) copy-start(bf16[4,2,512,512]{3,2,1,0:T(8,128)(2,1)} %constant.2.clone.refs_1_) | copy-start | bytes 12582916
  37.6 37.2 %copy-start.1 = (bf16[2,12,256,256]{3,2,1,0:T(8,128)(2,1)S(1)}, bf16[2,12,256,256]{3,2,1,0:T(8,128)(2,1)}, u32[]{:S(2)}) copy-start(bf16[2,12,256,256]{3,2,1,0:T(8,128)(2,1)} %refs_2_.1) | copy-start | bytes 9437188
